TPU v7x, 128 devices: a whole 4x4x4 slice. The times are simulated.
128 devices in a mesh: dp: 8 (over x, z_lo), vocab: 16 (over z_hi, y, core).
Axes of the slice: x: 4, y: 4, z: 4 (z_hi: 2, z_lo: 2; z = z_hi * 2 + z_lo), core: 2. Of those that a mesh axis runs over, the one named last changes fastest.
Arguments:
- hidden_rows: bfloat16 [768, 5120], P('dp')
- head_weight: bfloat16 [5120, 81920], P(None, ('dp', 'vocab')), may hold values from -0.625 to 0.625
- teacher_logits: bfloat16 [768, 81920], P(('dp', 'vocab'))
- upstream: float32 [768], replicated, may hold values from 2000 to 20000
- block_map: int32 [32], replicated, may hold values from 0 to 31, each once
- token_order: int32 [768], replicated, may hold values from 0 to 767, each once
Outputs:
- grad_head: bfloat16 [5120, 81920], P(None, ('dp', 'vocab'))
- grad_hidden: bfloat16 [768, 5120], P(('dp', 'vocab'))
Inputs may be any that keep to these rules, and one draw needn't show every extreme that they name: block_map is a permutation of the 32 blocks. token_order is a permutation of the 768 tokens.
All inputs are finite; a program needn't handle non-finite values.
Results may differ from a plain program's by a relative error of at most 0.0071.
Values may be sent and summed in bfloat16 or wider, within the bound.
A program may use at most 128 MiB of HBM per device.

v0:
```python
import jax
import jax.numpy as jnp
from jax import lax
from jax.sharding import PartitionSpec as P


def shards(hidden_rows, head_weight, teacher_logits, upstream, block_map, token_order):
    teacher_probs = jax.nn.softmax(teacher_logits.astype(jnp.float32), axis=1).astype(jnp.bfloat16)
    count = teacher_probs.shape[0]
    width = teacher_probs.shape[1]
    nblocks = block_map.shape[0]
    aligned = jnp.take(
        teacher_probs.reshape(count, nblocks, width // nblocks), block_map, axis=1
    ).reshape(count, width)
    aligned = lax.all_to_all(aligned, ("dp", "vocab"), split_axis=1, concat_axis=0, tiled=True)
    gathered = lax.all_gather(hidden_rows, "dp", axis=0, tiled=True)
    logits = jnp.dot(gathered, head_weight, preferred_element_type=jnp.float32)
    local_max = jnp.max(logits, axis=1)
    row_max = lax.pmax(local_max, ("dp", "vocab"))
    shifted = jnp.exp(logits - row_max[:, None])
    row_total = lax.psum(jnp.sum(shifted, axis=1), ("dp", "vocab"))
    logit_grad = (
        upstream[:, None] * (shifted / row_total[:, None] - aligned.astype(jnp.float32))
    ).astype(jnp.bfloat16)
    grad_head = lax.dot_general(
        gathered, logit_grad, (((0,), (0,)), ((), ())), preferred_element_type=jnp.float32
    )
    grad_head = grad_head.astype(jnp.bfloat16)
    picked = jnp.take(logit_grad, token_order, axis=0)
    grad_hidden = lax.psum_scatter(
        lax.dot_general(
            picked, head_weight, (((1,), (1,)), ((), ())), preferred_element_type=jnp.float32
        ),
        ("dp", "vocab"),
        scatter_dimension=0,
        tiled=True,
    ).astype(jnp.bfloat16)
    return (grad_head, grad_hidden)


def solution(mesh):
    in_specs = (P("dp", None), P(None, ("dp", "vocab")), P(("dp", "vocab"), None), P(), P(), P())
    out_specs = (P(None, ("dp", "vocab")), P(("dp", "vocab"), None))
    return jax.shard_map(shards, mesh=mesh, in_specs=in_specs, out_specs=out_specs, check_vma=False)
```

profile of v0, /device:TPU:1, one launch (start us, length us, event | category | flops | bytes accessed | tf_op | source)
XLA Modules:
  0.0 877.2 jit_solution(14299154939413372103)
XLA Ops:
  7.9 2.1 reduce_max.24
  15.0 11.9 %all-to-all-start = ((bf16[6,128,640]{2,0,1:T(8,128)(2,1)}), bf16[6,128,640]{2,0,1:T(8,128)(2,1)}, u32[]{:S(2)}, u32[]{:S(2)}) async-start(bf16[6,128,640]{2,0,1:T(8,128)(2,1)} %copy.16), calls=%async_computation | async-start | bytes 2621440 | tf_op jit(solution)/shard_map/all_to_all | solution.py:15
  27.0 32.5 %all-to-all-done = bf16[6,128,640]{2,0,1:T(8,128)(2,1)} async-done(((bf16[6,128,640]{2,0,1:T(8,128)(2,1)}), bf16[6,128,640]{2,0,1:T(8,128)(2,1)}, u32[]{:S(2)}, u32[]{:S(2)}) %all-to-all-start) | async-done | bytes 983072 | tf_op jit(solution)/shard_map/all_to_all | solution.py:15
  64.4 121.2 %all-gather.2.cloned.1.call-done = bf16[768,5120]{1,0:T(8,128)(2,1)} async-done(((bf16[96,5120]{1,0:T(8,128)(2,1)}), bf16[768,5120]{1,0:T(8,128)(2,1)}) %all-gather.2.cloned.1.call-update) | async-done | bytes 7864336 | tf_op jit(solution)/shard_map/all_gather | solution.py:16
  185.5 11.7 %fusion.10 = (f32[768]{0:T(1024)S(1)}, f32[768,640]{0,1:T(8,128)}) fusion(bf16[768,5120]{1,0:T(8,128)(2,1)} %all-gather.2.cloned.1.call-done, bf16[5120,640]{1,0:T(8,128)(2,1)} %param.7), kind=kOutput, calls=%fused_computation.25 | convolution fusion | flops 5033655296 | bytes 16387072 | tf_op jit(solution)/shard_map/dot_general | solution.py:17
  197.2 68.1 %pmax.7 = f32[768]{0:T(1024)S(1)} all-reduce(f32[768]{0:T(1024)S(1)} %get-tuple-element.39), channel_id=1, replica_groups=mesh['dp'=8,'vocab'=16] {'dp','vocab'}, use_global_device_ids=true, to_apply=%region_1.0 | all-reduce | flops 768 | bytes 6144 | tf_op jit(solution)/shard_map/pmax | solution.py:19
  267.2 63.8 %psum.7 = f32[768]{0:T(1024)S(1)} all-reduce(f32[768]{0:T(1024)S(1)} %fusion.3), channel_id=1, replica_groups=mesh['dp'=8,'vocab'=16] {'dp','vocab'}, use_global_device_ids=true, to_apply=%region_3.4 | all-reduce | flops 768 | bytes 6144 | tf_op jit(solution)/shard_map/psum | solution.py:21
  333.6 2.8 gather_fusion.1
  336.4 12.1 %fusion.4 = f32[768,5120]{1,0:T(8,128)} fusion(bf16[5120,640]{1,0:T(8,128)(2,1)} %param.7, bf16[768,640]{1,0:T(8,128)(2,1)S(1)} %gather_fusion.1, pred[768]{0:T(1024)(128)(4,1)S(1)} %compare_and_fusion), kind=kOutput, calls=%fused_computation.11 | convolution fusion | flops 5033656320 | bytes 23266048 | tf_op jit(solution)/shard_map/dot_general | solution.py:31
  348.5 359.6 %fusion = f32[8,5120]{1,0:T(8,128)S(1)} fusion(f32[768,5120]{1,0:T(8,128)} %fusion.4), kind=kCustom, calls=%all-reduce-scatter | all-reduce-scatter fusion | flops 5242881 | bytes 15892480
  719.9 13.8 %collective-permute-start.22 = (bf16[8,5120]{1,0:T(8,128)(2,1)S(1)}, bf16[8,5120]{1,0:T(8,128)(2,1)S(1)}, u32[]{:S(2)}, u32[]{:S(2)}) collective-permute-start(bf16[8,5120]{1,0:T(8,128)(2,1)S(1)} %convert.72), channel_id=1, source_target_pairs={{0,23},{1,24},{2,25},{3,26},{4,27},{5,28},{6,29},{7,30},{8,31},{9,... | collective-permute-start | bytes 245768
  733.8 3.8 collective-permute-start.21
  737.6 2.8 collective-permute-start.20
  740.4 2.2 collective-permute-start.19
  742.7 3.4 collective-permute-start.18
  746.1 2.5 collective-permute-start.17
  750.1 2.1 collective-permute-start.15
  752.3 2.5 collective-permute-start.14
  754.8 5.5 collective-permute-start.13
  760.4 2.6 collective-permute-start.12
  763.0 2.2 collective-permute-start.11
  765.3 4.4 collective-permute-start.10
  771.8 2.3 collective-permute-start.8
  775.6 4.2 collective-permute-start.6
  779.8 2.2 collective-permute-start.5
  782.1 4.5 collective-permute-start.4
  786.7 3.2 collective-permute-start.3
  789.9 5.8 collective-permute-start.2
  797.6 2.1 collective-permute-start
  799.7 10.4 %fusion.1 = bf16[5120,640]{0,1:T(8,128)(2,1)} fusion(bf16[768,640]{0,1:T(8,128)(2,1)S(1)} %multiply_convert_fusion, bf16[768,5120]{1,0:T(8,128)(2,1)} %all-gather.2.cloned.1.call-done), kind=kOutput, calls=%fused_computation.3 | convolution fusion | flops 5036441600 | bytes 15400960 | tf_op jit(solution)/shard_map/dot_general | solution.py:25
  810.3 9.5 %copy.19 = bf16[5120,640]{1,0:T(8,128)(2,1)} copy(bf16[5120,640]{0,1:T(8,128)(2,1)} %fusion.1) | data formatting | bytes 13107200
  820.4 49.3 %concatenate = bf16[262,5120]{1,0:T(8,128)(2,1)S(1)} concatenate(bf16[6,5120]{1,0:T(8,128)(2,1)S(1)} %collective-permute-done.31, bf16[8,5120]{1,0:T(8,128)(2,1)S(1)} %collective-permute-done.30, bf16[8,5120]{1,0:T(8,128)(2,1)S(1)} %collective-permute-done.29, bf16[8,5120]{1,0:T(8,128)(2,1)S(1)} %collective-permute-done.28, bf16[8,5120]{1,0:T(8,128)(2,1)S(1)} %collective-permute-done.27, ...), dimensions={0} | concatenate | bytes 5447680
  (126 shorter events, 35.0 us)
Async XLA Ops:
  7.2 178.3 %all-gather.2.cloned.1.call-start = ((), (), s32[]{:S(2)}) async-start(), calls=%async_computation.1 | async-start | bytes 8847360 | tf_op jit(solution)/shard_map/all_gather | solution.py:16
  15.0 44.5 %all-to-all-start = ((bf16[6,128,640]{2,0,1:T(8,128)(2,1)}), bf16[6,128,640]{2,0,1:T(8,128)(2,1)}, u32[]{:S(2)}, u32[]{:S(2)}) async-start(bf16[6,128,640]{2,0,1:T(8,128)(2,1)} %copy.16), calls=%async_computation | async-start | bytes 2621440 | tf_op jit(solution)/shard_map/all_to_all | solution.py:15
  708.1 7.9 collective-permute-start.30
  712.0 6.5 collective-permute-start.28
  713.3 6.6 collective-permute-start.27
  714.6 19.1 %collective-permute-start.26 = (bf16[8,5120]{1,0:T(8,128)(2,1)S(1)}, bf16[8,5120]{1,0:T(8,128)(2,1)S(1)}, u32[]{:S(2)}, u32[]{:S(2)}) collective-permute-start(bf16[8,5120]{1,0:T(8,128)(2,1)S(1)} %convert.72), channel_id=1, source_target_pairs={{0,27},{1,28},{2,29},{3,30},{4,31},{5,32},{6,33},{7,34},{8,35},{9,... | collective-permute-start | bytes 245768
  716.0 21.6 %collective-permute-start.25 = (bf16[8,5120]{1,0:T(8,128)(2,1)S(1)}, bf16[8,5120]{1,0:T(8,128)(2,1)S(1)}, u32[]{:S(2)}, u32[]{:S(2)}) collective-permute-start(bf16[8,5120]{1,0:T(8,128)(2,1)S(1)} %convert.72), channel_id=1, source_target_pairs={{0,26},{1,27},{2,28},{3,29},{4,30},{5,31},{6,32},{7,33},{8,34},{9,... | collective-permute-start | bytes 245768
  717.3 23.1 %collective-permute-start.24 = (bf16[8,5120]{1,0:T(8,128)(2,1)S(1)}, bf16[8,5120]{1,0:T(8,128)(2,1)S(1)}, u32[]{:S(2)}, u32[]{:S(2)}) collective-permute-start(bf16[8,5120]{1,0:T(8,128)(2,1)S(1)} %convert.72), channel_id=1, source_target_pairs={{0,25},{1,26},{2,27},{3,28},{4,29},{5,30},{6,31},{7,32},{8,33},{9,... | collective-permute-start | bytes 245768
  718.6 24.1 %collective-permute-start.23 = (bf16[8,5120]{1,0:T(8,128)(2,1)S(1)}, bf16[8,5120]{1,0:T(8,128)(2,1)S(1)}, u32[]{:S(2)}, u32[]{:S(2)}) collective-permute-start(bf16[8,5120]{1,0:T(8,128)(2,1)S(1)} %convert.72), channel_id=1, source_target_pairs={{0,24},{1,25},{2,26},{3,27},{4,28},{5,29},{6,30},{7,31},{8,32},{9,... | collective-permute-start | bytes 245768
  719.9 26.2 %collective-permute-start.22 = (bf16[8,5120]{1,0:T(8,128)(2,1)S(1)}, bf16[8,5120]{1,0:T(8,128)(2,1)S(1)}, u32[]{:S(2)}, u32[]{:S(2)}) collective-permute-start(bf16[8,5120]{1,0:T(8,128)(2,1)S(1)} %convert.72), channel_id=1, source_target_pairs={{0,23},{1,24},{2,25},{3,26},{4,27},{5,28},{6,29},{7,30},{8,31},{9,... | collective-permute-start | bytes 245768
  733.8 14.9 %collective-permute-start.21 = (bf16[8,5120]{1,0:T(8,128)(2,1)S(1)}, bf16[8,5120]{1,0:T(8,128)(2,1)S(1)}, u32[]{:S(2)}, u32[]{:S(2)}) collective-permute-start(bf16[8,5120]{1,0:T(8,128)(2,1)S(1)} %convert.72), channel_id=1, source_target_pairs={{0,22},{1,23},{2,24},{3,25},{4,26},{5,27},{6,28},{7,29},{8,30},{9,... | collective-permute-start | bytes 245768
  737.6 12.5 %collective-permute-start.20 = (bf16[8,5120]{1,0:T(8,128)(2,1)S(1)}, bf16[8,5120]{1,0:T(8,128)(2,1)S(1)}, u32[]{:S(2)}, u32[]{:S(2)}) collective-permute-start(bf16[8,5120]{1,0:T(8,128)(2,1)S(1)} %convert.72), channel_id=1, source_target_pairs={{0,21},{1,22},{2,23},{3,24},{4,25},{5,26},{6,27},{7,28},{8,29},{9,... | collective-permute-start | bytes 245768
  740.4 11.8 %collective-permute-start.19 = (bf16[8,5120]{1,0:T(8,128)(2,1)S(1)}, bf16[8,5120]{1,0:T(8,128)(2,1)S(1)}, u32[]{:S(2)}, u32[]{:S(2)}) collective-permute-start(bf16[8,5120]{1,0:T(8,128)(2,1)S(1)} %convert.72), channel_id=1, source_target_pairs={{0,20},{1,21},{2,22},{3,23},{4,24},{5,25},{6,26},{7,27},{8,28},{9,... | collective-permute-start | bytes 245768
  742.7 12.2 %collective-permute-start.18 = (bf16[8,5120]{1,0:T(8,128)(2,1)S(1)}, bf16[8,5120]{1,0:T(8,128)(2,1)S(1)}, u32[]{:S(2)}, u32[]{:S(2)}) collective-permute-start(bf16[8,5120]{1,0:T(8,128)(2,1)S(1)} %convert.72), channel_id=1, source_target_pairs={{0,19},{1,20},{2,21},{3,22},{4,23},{5,24},{6,25},{7,26},{8,27},{9,... | collective-permute-start | bytes 245768
  746.1 14.2 %collective-permute-start.17 = (bf16[8,5120]{1,0:T(8,128)(2,1)S(1)}, bf16[8,5120]{1,0:T(8,128)(2,1)S(1)}, u32[]{:S(2)}, u32[]{:S(2)}) collective-permute-start(bf16[8,5120]{1,0:T(8,128)(2,1)S(1)} %convert.72), channel_id=1, source_target_pairs={{0,18},{1,19},{2,20},{3,21},{4,22},{5,23},{6,24},{7,25},{8,26},{9,... | collective-permute-start | bytes 245768
  748.7 14.4 %collective-permute-start.16 = (bf16[8,5120]{1,0:T(8,128)(2,1)S(1)}, bf16[8,5120]{1,0:T(8,128)(2,1)S(1)}, u32[]{:S(2)}, u32[]{:S(2)}) collective-permute-start(bf16[8,5120]{1,0:T(8,128)(2,1)S(1)} %convert.72), channel_id=1, source_target_pairs={{0,17},{1,18},{2,19},{3,20},{4,21},{5,22},{6,23},{7,24},{8,25},{9,... | collective-permute-start | bytes 245768
  750.1 15.2 %collective-permute-start.15 = (bf16[8,5120]{1,0:T(8,128)(2,1)S(1)}, bf16[8,5120]{1,0:T(8,128)(2,1)S(1)}, u32[]{:S(2)}, u32[]{:S(2)}) collective-permute-start(bf16[8,5120]{1,0:T(8,128)(2,1)S(1)} %convert.72), channel_id=1, source_target_pairs={{0,16},{1,17},{2,18},{3,19},{4,20},{5,21},{6,22},{7,23},{8,24},{9,... | collective-permute-start | bytes 245768
  752.3 17.4 %collective-permute-start.14 = (bf16[8,5120]{1,0:T(8,128)(2,1)S(1)}, bf16[8,5120]{1,0:T(8,128)(2,1)S(1)}, u32[]{:S(2)}, u32[]{:S(2)}) collective-permute-start(bf16[8,5120]{1,0:T(8,128)(2,1)S(1)} %convert.72), channel_id=1, source_target_pairs={{0,15},{1,16},{2,17},{3,18},{4,19},{5,20},{6,21},{7,22},{8,23},{9,... | collective-permute-start | bytes 245768
  754.8 17.0 %collective-permute-start.13 = (bf16[8,5120]{1,0:T(8,128)(2,1)S(1)}, bf16[8,5120]{1,0:T(8,128)(2,1)S(1)}, u32[]{:S(2)}, u32[]{:S(2)}) collective-permute-start(bf16[8,5120]{1,0:T(8,128)(2,1)S(1)} %convert.72), channel_id=1, source_target_pairs={{0,14},{1,15},{2,16},{3,17},{4,18},{5,19},{6,20},{7,21},{8,22},{9,... | collective-permute-start | bytes 245768
  760.4 13.8 %collective-permute-start.12 = (bf16[8,5120]{1,0:T(8,128)(2,1)S(1)}, bf16[8,5120]{1,0:T(8,128)(2,1)S(1)}, u32[]{:S(2)}, u32[]{:S(2)}) collective-permute-start(bf16[8,5120]{1,0:T(8,128)(2,1)S(1)} %convert.72), channel_id=1, source_target_pairs={{0,13},{1,14},{2,15},{3,16},{4,17},{5,18},{6,19},{7,20},{8,21},{9,... | collective-permute-start | bytes 245768
  763.0 12.6 %collective-permute-start.11 = (bf16[8,5120]{1,0:T(8,128)(2,1)S(1)}, bf16[8,5120]{1,0:T(8,128)(2,1)S(1)}, u32[]{:S(2)}, u32[]{:S(2)}) collective-permute-start(bf16[8,5120]{1,0:T(8,128)(2,1)S(1)} %convert.72), channel_id=1, source_target_pairs={{0,12},{1,13},{2,14},{3,15},{4,16},{5,17},{6,18},{7,19},{8,20},{9,... | collective-permute-start | bytes 245768
  765.3 14.5 %collective-permute-start.10 = (bf16[8,5120]{1,0:T(8,128)(2,1)S(1)}, bf16[8,5120]{1,0:T(8,128)(2,1)S(1)}, u32[]{:S(2)}, u32[]{:S(2)}) collective-permute-start(bf16[8,5120]{1,0:T(8,128)(2,1)S(1)} %convert.72), channel_id=1, source_target_pairs={{0,11},{1,12},{2,13},{3,14},{4,15},{5,16},{6,17},{7,18},{8,19},{9,... | collective-permute-start | bytes 245768
  769.7 12.4 %collective-permute-start.9 = (bf16[8,5120]{1,0:T(8,128)(2,1)S(1)}, bf16[8,5120]{1,0:T(8,128)(2,1)S(1)}, u32[]{:S(2)}, u32[]{:S(2)}) collective-permute-start(bf16[8,5120]{1,0:T(8,128)(2,1)S(1)} %convert.72), channel_id=1, source_target_pairs={{0,10},{1,11},{2,12},{3,13},{4,14},{5,15},{6,16},{7,17},{8,18},{9,... | collective-permute-start | bytes 245768
  771.8 14.8 %collective-permute-start.8 = (bf16[8,5120]{1,0:T(8,128)(2,1)S(1)}, bf16[8,5120]{1,0:T(8,128)(2,1)S(1)}, u32[]{:S(2)}, u32[]{:S(2)}) collective-permute-start(bf16[8,5120]{1,0:T(8,128)(2,1)S(1)} %convert.72), channel_id=1, source_target_pairs={{0,9},{1,10},{2,11},{3,12},{4,13},{5,14},{6,15},{7,16},{8,17},{9,1... | collective-permute-start | bytes 245768
  774.2 15.7 %collective-permute-start.7 = (bf16[8,5120]{1,0:T(8,128)(2,1)S(1)}, bf16[8,5120]{1,0:T(8,128)(2,1)S(1)}, u32[]{:S(2)}, u32[]{:S(2)}) collective-permute-start(bf16[8,5120]{1,0:T(8,128)(2,1)S(1)} %convert.72), channel_id=1, source_target_pairs={{0,8},{1,9},{2,10},{3,11},{4,12},{5,13},{6,14},{7,15},{8,16},{9,17... | collective-permute-start | bytes 245768
  775.6 20.0 %collective-permute-start.6 = (bf16[8,5120]{1,0:T(8,128)(2,1)S(1)}, bf16[8,5120]{1,0:T(8,128)(2,1)S(1)}, u32[]{:S(2)}, u32[]{:S(2)}) collective-permute-start(bf16[8,5120]{1,0:T(8,128)(2,1)S(1)} %convert.72), channel_id=1, source_target_pairs={{0,7},{1,8},{2,9},{3,10},{4,11},{5,12},{6,13},{7,14},{8,15},{9,16}... | collective-permute-start | bytes 245768
  779.8 17.7 %collective-permute-start.5 = (bf16[8,5120]{1,0:T(8,128)(2,1)S(1)}, bf16[8,5120]{1,0:T(8,128)(2,1)S(1)}, u32[]{:S(2)}, u32[]{:S(2)}) collective-permute-start(bf16[8,5120]{1,0:T(8,128)(2,1)S(1)} %convert.72), channel_id=1, source_target_pairs={{0,6},{1,7},{2,8},{3,9},{4,10},{5,11},{6,12},{7,13},{8,14},{9,15},... | collective-permute-start | bytes 245768
  782.1 37.7 %collective-permute-start.4 = (bf16[8,5120]{1,0:T(8,128)(2,1)S(1)}, bf16[8,5120]{1,0:T(8,128)(2,1)S(1)}, u32[]{:S(2)}, u32[]{:S(2)}) collective-permute-start(bf16[8,5120]{1,0:T(8,128)(2,1)S(1)} %convert.72), channel_id=1, source_target_pairs={{0,5},{1,6},{2,7},{3,8},{4,9},{5,10},{6,11},{7,12},{8,13},{9,14},{... | collective-permute-start | bytes 245768
  786.7 33.1 %collective-permute-start.3 = (bf16[8,5120]{1,0:T(8,128)(2,1)S(1)}, bf16[8,5120]{1,0:T(8,128)(2,1)}, u32[]{:S(2)}, u32[]{:S(2)}) collective-permute-start(bf16[8,5120]{1,0:T(8,128)(2,1)S(1)} %convert.72), channel_id=1, source_target_pairs={{0,4},{1,5},{2,6},{3,7},{4,8},{5,9},{6,10},{7,11},{8,12},{9,13},{1... | collective-permute-start | bytes 245768
  789.9 29.9 %collective-permute-start.2 = (bf16[8,5120]{1,0:T(8,128)(2,1)S(1)}, bf16[8,5120]{1,0:T(8,128)(2,1)}, u32[]{:S(2)}, u32[]{:S(2)}) collective-permute-start(bf16[8,5120]{1,0:T(8,128)(2,1)S(1)} %convert.72), channel_id=1, source_target_pairs={{0,3},{1,4},{2,5},{3,6},{4,7},{5,8},{6,9},{7,10},{8,11},{9,12},{10... | collective-permute-start | bytes 245768
  795.6 24.1 %collective-permute-start.1 = (bf16[8,5120]{1,0:T(8,128)(2,1)S(1)}, bf16[8,5120]{1,0:T(8,128)(2,1)}, u32[]{:S(2)}, u32[]{:S(2)}) collective-permute-start(bf16[8,5120]{1,0:T(8,128)(2,1)S(1)} %convert.72), channel_id=1, source_target_pairs={{0,2},{1,3},{2,4},{3,5},{4,6},{5,7},{6,8},{7,9},{8,10},{9,11},{10,... | collective-permute-start | bytes 245768
  797.6 22.8 %collective-permute-start = (bf16[8,5120]{1,0:T(8,128)(2,1)S(1)}, bf16[8,5120]{1,0:T(8,128)(2,1)}, u32[]{:S(2)}, u32[]{:S(2)}) collective-permute-start(bf16[8,5120]{1,0:T(8,128)(2,1)S(1)} %convert.72), channel_id=1, source_target_pairs={{0,1},{1,2},{2,3},{3,4},{4,5},{5,6},{6,7},{7,8},{8,9},{9,10},{10,1... | collective-permute-start | bytes 245768
  (29 other events, 1305.4 us)
Sparse Core Ops, SparseCore 0:
  9.7 175.8 all-gather.1
where the time goes:
time: 882 us; the launch traced here: 877 us
  blocking collectives  492 us (56%)
  waiting for transfers between devices  154 us (17%)
  starting transfers between devices  103 us (12%)
  local copies, waits for them, and re-layouts  70.2 us (8%)
  matrix products  34.2 us (4%)
  between operations  15 us (2%)
  other arithmetic  9.07 us (1%)
    unnamed x1, blocking collectives  360 us
    all_gather x1, waiting for transfers between devices, shards(): gathered = lax.all_gather(hidden_rows, 'dp', axis=0, tiled=True)  121 us
    unnamed x32, starting transfers between devices  90.9 us
    pmax x1, blocking collectives, shards(): row_max = lax.pmax(local_max, ('dp', 'vocab'))  68.1 us
    psum x1, blocking collectives, shards(): row_total = lax.psum(jnp.sum(shifted, axis=1), ('dp', 'vocab'))  63.8 us
    unnamed x57, local copies, waits for them, and re-layouts  59.5 us
    all_to_all x1, waiting for transfers between devices, shards(): lax.all_to_all(aligned, ('dp', 'vocab'), split_axis=1, concat_axis=0, til...  32.5 us
  transfers between devices with their start and end apart: 34, of which 2 were waited for; matrix products, arithmetic and copies ran while one was open for 4% of the time, Pallas kernels for 0%

commit v1 on v0

v1 whole, which is shorter than its diff:
```python
import jax
import jax.numpy as jnp
from jax import lax
from jax.experimental import pallas as pl
from jax.experimental.pallas import tpu as pltpu
from jax.sharding import PartitionSpec as P

MESH = pl.DeviceIdType.MESH
F32 = jnp.float32
BF16 = jnp.bfloat16
HALF = 2560
XW, YW, ZW = 512, 256, 1024
Y0, Z0 = 512, 1536
LANES = ((0, (512, 384)), (896, (512, 384)), (1792, (384, 384)))


def device(x, y, z, c):
    return (x * 2 + lax.rem(z, 2), (z // 2) * 8 + y * 2 + c)


def teacher_kernel(bmap, t_ref, o_ref):
    width = 2560

    def top(j, m):
        cols = pl.ds(pl.multiple_of(j * width, width), width)
        return jnp.maximum(m, jnp.max(t_ref[:, cols].astype(F32), axis=1, keepdims=True))

    m = lax.fori_loop(0, 32, top, jnp.full((6, 1), -jnp.inf, F32))

    def add(j, s):
        cols = pl.ds(pl.multiple_of(j * width, width), width)
        return s + jnp.sum(jnp.exp(t_ref[:, cols].astype(F32) - m), axis=1, keepdims=True)

    s = lax.fori_loop(0, 32, add, jnp.zeros((6, 1), F32))
    pad = jnp.zeros((2, 128), F32)

    def block(j, carry):
        cols = pl.ds(pl.multiple_of(bmap[j] * width, width), width)
        p = jnp.exp(t_ref[:, cols].astype(F32) - m) / s
        for k in range(4):
            rows = [p[:, 640 * k + 128 * i : 640 * k + 128 * i + 128] for i in range(5)]
            o_ref[4 * j + k] = jnp.concatenate(rows + [pad], axis=0).astype(BF16)
        return carry

    lax.fori_loop(0, 32, block, 0)


def head_kernel(
    hid, w, tea, ups, tok, gh, gx,
    hb, wb, ws, acc, qb, rt, g, st0, st1, st2, perm, gp, gs, ghb, fin, fs,
    t00, t01, t10, t11, t20, t21, a00, a01, a10, a11, a20, a21,
    u00, u01, u10, u11, u20, u21, b00, b01, b10, b11, b20, b21,
    v00, v01, v10, v11, v20, v21, c00, c01, c10, c11, c20, c21,
    ss, rs, ls, tss, trs,
):
    tps = ((t00, t01), (t10, t11), (t20, t21))
    ras = ((a00, a01), (a10, a11), (a20, a21))
    tbs = ((u00, u01), (u10, u11), (u20, u21))
    rbs = ((b00, b01), (b10, b11), (b20, b21))
    tcs = ((v00, v01), (v10, v11), (v20, v21))
    rcs = ((c00, c01), (c10, c11), (c20, c21))
    dp = lax.axis_index("dp")
    vo = lax.axis_index("vocab")
    x, zl = dp // 2, lax.rem(dp, 2)
    zh, y, c = vo // 8, lax.rem(vo // 2, 4), lax.rem(vo, 2)
    z = zh * 2 + zl
    o = 1 - c
    me = dp * 16 + vo

    def rot(v, d):
        return lax.rem(v + d, 4)

    def xn(d):
        return device(rot(x, d), y, z, c)

    def yn(d):
        return device(x, rot(y, d), z, c)

    def zn(d):
        return device(x, y, rot(z, d), c)

    sib = device(x, y, z, o)
    sent = []

    def send(src, dst, to):
        k = len(sent)
        cp = pltpu.make_async_remote_copy(
            src_ref=src, dst_ref=dst, send_sem=ss.at[k], recv_sem=rs.at[k],
            device_id=to, device_id_type=MESH,
        )
        cp.start()
        sent.append(cp)
        return cp

    def arrive(*cps):
        for cp in cps:
            cp.wait_recv()

    q0, qo = 2 * zl, 2 * (1 - zl)
    mine = pl.multiple_of(HALF * c, 128)
    own = (
        pltpu.make_async_copy(hid.at[:, :, pl.ds(mine, XW)], hb.at[c, x, pl.ds(q0, 2), :, pl.ds(0, XW)], ls.at[0]),
        pltpu.make_async_copy(
            hid.at[:, :, pl.ds(pl.multiple_of(mine + Y0 + YW * y, 128), YW)],
            hb.at[c, x, pl.ds(q0, 2), :, pl.ds(pl.multiple_of(Y0 + YW * y, 128), YW)], ls.at[14]),
        pltpu.make_async_copy(
            hid.at[zh, :, pl.ds(pl.multiple_of(mine + Z0, 128), ZW)],
            hb.at[c, x, q0 + zh, :, pl.ds(Z0, ZW)], ls.at[15]),
    )
    for cp in own:
        cp.start()
    other = pltpu.make_async_copy(
        hid.at[:, :, pl.ds(pl.multiple_of(HALF * o, 128), XW)],
        hb.at[o, x, pl.ds(q0, 2), :, pl.ds(0, XW)], ls.at[1])
    other.start()
    wcopy = pltpu.make_async_copy(w, wb, ls.at[2])
    wcopy.start()
    tcopy = pltpu.make_async_copy(tea.at[me], rt.at[me], ls.at[3])
    tcopy.start()

    bar = pltpu.get_barrier_semaphore()

    def greet(i, carry):
        t = lax.rem(me + i, 128)
        pl.semaphore_signal(bar, inc=1, device_id=(t // 16, lax.rem(t, 16)), device_id_type=MESH)
        return carry

    lax.fori_loop(1, 128, greet, 0)
    pl.semaphore_wait(bar, 127)
    for cp in own:
        cp.wait()

    def ysl(yy):
        return pl.ds(pl.multiple_of(Y0 + YW * yy, 128), YW)

    def zq(zz):
        return 2 * lax.rem(zz, 2) + zz // 2

    def same(ref, to):
        return send(ref, ref, to)

    xs, zs = pl.ds(0, XW), pl.ds(Z0, ZW)
    px = (same(hb.at[c, x, q0, :, xs], zn(1)), same(hb.at[c, x, q0 + 1, :, xs], zn(3)))
    py = (same(hb.at[c, x, q0, :, ysl(y)], zn(1)), same(hb.at[c, x, q0 + 1, :, ysl(y)], zn(3)))
    z1 = [same(hb.at[c, x, zq(z), :, zs], xn(d)) for d in (1, 3, 2)]
    y1 = [same(hb.at[c, x, pl.ds(q0, 2), :, ysl(y)], xn(d)) for d in (1, 3, 2)]
    x1 = [same(hb.at[c, x, pl.ds(q0, 2), :, xs], xn(d)) for d in (1, 3, 2)]
    wx = send(w.at[o], ws, sib)
    arrive(*py)
    y2 = [same(hb.at[c, x, pl.ds(qo, 2), :, ysl(y)], xn(d)) for d in (1, 3, 2)]
    arrive(*px)
    x2 = [same(hb.at[c, x, pl.ds(qo, 2), :, xs], xn(d)) for d in (1, 3, 2)]
    dx0 = same(hb.at[c, x, pl.ds(qo, 2), :, xs], sib)
    arrive(*z1)
    z2 = [same(hb.at[c, :, zq(z), :, zs], zn(d)) for d in (1, 3, 2)]
    dz0 = same(hb.at[c, :, zq(z), :, zs], sib)
    arrive(*y1)
    arrive(*y2)
    y3 = [same(hb.at[c, :, :, :, ysl(y)], yn(d)) for d in (1, 3, 2)]
    dy0 = same(hb.at[c, :, :, :, ysl(y)], sib)

    def give(i, carry):
        t = lax.rem(me + i, 128)
        pltpu.make_async_remote_copy(
            src_ref=tea.at[t], dst_ref=rt.at[me], send_sem=tss, recv_sem=trs,
            device_id=(t // 16, lax.rem(t, 16)), device_id_type=MESH,
        ).start()
        return carry

    lax.fori_loop(1, 128, give, 0)

    acc[...] = jnp.zeros_like(acc)

    def mul_x(h, xx):
        lhs = hb[h, xx, :, :, xs].reshape(192, XW)
        rows = pl.ds(pl.multiple_of(192 * xx, 64), 192)
        acc[rows, :] += jnp.dot(lhs, wb[h, xs, :], preferred_element_type=F32)

    def mul_y(h, yy):
        lhs = hb[h, :, :, :, ysl(yy)].reshape(768, YW)
        acc[...] += jnp.dot(lhs, wb[h, ysl(yy), :], preferred_element_type=F32)

    def mul_z(h, zz):
        q = zq(zz)
        lhs = hb[h, :, q, :, zs].reshape(192, ZW)
        res = jnp.dot(lhs, wb[h, zs, :], preferred_element_type=F32)
        for xx in range(4):
            rows = pl.ds(pl.multiple_of(192 * xx + 48 * q, 16), 48)
            acc[rows, :] += res[48 * xx : 48 * xx + 48]

    for p in range(3):
        for a in range(6):
            i = lax.broadcasted_iota(jnp.int32, (128, 1), 0) + 128 * a
            n = (i * 43691) >> 19
            k = i - 12 * n
            core = jnp.where(k >= 6, 1, 0)
            first, second, third = n >> 4, (n >> 2) & 3, n & 3
            rx, ry, rz = ((first, second, third), (third, first, second), (second, third, first))[p]
            row = 6 * ((rx * 2 + (rz & 1)) * 16 + (rz >> 1) * 8 + ry * 2 + core) + k - 6 * core
            col = lax.broadcasted_iota(jnp.int32, (128, 768), 1)
            token = jnp.sum(jnp.where(col == row, tok[...], 0.0), axis=1, keepdims=True)
            perm[p, 128 * a : 128 * a + 128, :] = jnp.where(col.astype(F32) == token, 1.0, 0.0).astype(BF16)

    wcopy.wait()
    mul_x(c, x)
    mul_z(c, z)
    mul_y(c, y)
    other.wait()
    arrive(dx0)
    mul_x(o, x)
    arrive(dz0)
    mul_z(o, z)
    arrive(dy0)
    mul_y(o, y)
    dxs, dzs, dys = [], [], []
    for i, d in enumerate((3, 1, 2)):
        arrive(x1[i], x2[i])
        dxs.append(same(hb.at[c, rot(x, d), :, :, xs], sib))
        mul_x(c, rot(x, d))
    for i, d in enumerate((3, 1, 2)):
        arrive(z2[i])
        dzs.append(same(hb.at[c, :, zq(rot(z, d)), :, zs], sib))
        arrive(y3[i])
        dys.append(same(hb.at[c, :, :, :, ysl(rot(y, d))], sib))
        arrive(dxs[i])
        mul_x(o, rot(x, d))
        mul_z(c, rot(z, d))
        mul_y(c, rot(y, d))
        if i > 0:
            e = (3, 1, 2)[i - 1]
            arrive(dzs[i - 1])
            mul_z(o, rot(z, e))
            arrive(dys[i - 1])
            mul_y(o, rot(y, e))
    arrive(dzs[2])
    mul_z(o, rot(z, 2))
    arrive(dys[2])
    mul_y(o, rot(y, 2))

    eye = lax.broadcasted_iota(jnp.int32, (128, 128), 0) == lax.broadcasted_iota(jnp.int32, (128, 128), 1)
    st0[...] = jnp.zeros_like(st0)

    def to_row(v):
        return jnp.sum(jnp.where(eye, v, 0.0), axis=0, keepdims=True)

    def to_col(v):
        return jnp.sum(jnp.where(eye, v, 0.0), axis=1, keepdims=True)

    for a in range(6):
        rows = slice(128 * a, 128 * a + 128)
        l = acc[rows, :]
        m = jnp.max(l, axis=1, keepdims=True)
        e = jnp.exp(l - m)
        acc[rows, :] = e
        st0[a : a + 1, :] = to_row(m)
        st0[8 + a : 9 + a, :] = to_row(jnp.sum(e, axis=1, keepdims=True))

    def merge(first, ref, n):
        m = first[0:8]
        for k in range(1, n):
            m = jnp.maximum(m, ref[k, 0:8, :])
        s = first[8:16] * jnp.exp(first[0:8] - m)
        for k in range(1, n):
            s += ref[k, 8:16, :] * jnp.exp(ref[k, 0:8, :] - m)
        return m, s

    cps = []
    for d in range(4):
        for e in range(2):
            if d + e > 0:
                to = device(rot(x, d), y, z, c if e == 0 else o)
                cps.append(send(st0, st1.at[2 * d + e], to))
    arrive(*cps)
    m, s = merge(st0[...], st1, 8)
    st2[0, 0:8, :] = m
    st2[0, 8:16, :] = s
    cps = []
    for d in range(4):
        for e in range(4):
            if d + e > 0:
                cps.append(send(st2.at[0], st2.at[4 * d + e], device(x, rot(y, d), rot(z, e), c)))

    tcopy.wait()
    whole = pltpu.make_async_remote_copy(
        src_ref=tea.at[pl.ds(0, 127)], dst_ref=rt.at[pl.ds(0, 127)], send_sem=tss, recv_sem=trs,
        device_id=sib, device_id_type=MESH,
    )
    whole.wait_recv()
    i = lax.broadcasted_iota(jnp.int32, (240, 1), 0)
    j = (i * 1366) >> 16
    k = i - 48 * j
    t = (k * 43) >> 8
    want = t * 32 + j * 6 + (k - 6 * t)
    pick = jnp.where(lax.broadcasted_iota(jnp.int32, (240, 256), 1) == want, 1.0, 0.0).astype(BF16)

    def place(n, carry):
        src = rt[pl.ds(8 * n, 8)].reshape(256, 128)
        res = jnp.dot(pick, src, preferred_element_type=F32).astype(BF16)
        for jj in range(5):
            qb[pl.ds(pl.multiple_of(48 * n, 16), 48), 128 * jj : 128 * jj + 128] = res[48 * jj : 48 * jj + 48]
        return carry

    lax.fori_loop(0, 16, place, 0)

    arrive(*cps)
    m, s = merge(st2[0], st2, 16)
    scale = ups[...] * jnp.exp(st0[0:6, :] - m[0:6]) / s[0:6]
    for a in range(6):
        rows = slice(128 * a, 128 * a + 128)
        sc = to_col(scale[a : a + 1, :])
        uc = to_col(ups[a : a + 1, :])
        g[rows, :] = (acc[rows, :] * sc - uc * qb[rows, :].astype(F32)).astype(BF16)

    gsend = []
    for p in range(3):
        for a in range(3):
            rows = slice(256 * a, 256 * a + 256)
            gp[p, rows, :] = jnp.dot(perm[p, rows, :], g[...], preferred_element_type=F32).astype(BF16)
        gsend.append(send(gp.at[p], gs.at[p], sib))
    wx.wait_recv()

    co = (x, y, z)
    near = (xn, yn, zn)
    nt = (((1,), (1,)), ((), ()))
    sa, sb, sc3 = {}, {}, {}

    def head_part(n):
        h, k = n // 5, n % 5
        lhs = hb[h, :, :, :, 512 * k : 512 * k + 512].reshape(768, 512)
        res = lax.dot_general(lhs, g[...], (((0,), (0,)), ((), ())), preferred_element_type=F32)
        ghb[512 * n : 512 * n + 512, :] = res.astype(BF16)
        cp = pltpu.make_async_copy(ghb.at[pl.ds(512 * n, 512)], gh.at[pl.ds(512 * n, 512)], ls.at[4 + n])
        cp.start()
        return cp

    def stage_a(p, k):
        start, widths = LANES[p]
        wd = widths[k]
        at = start + (widths[0] if k else 0)
        wo = wb[c, at : at + wd, :]
        wt = ws[at : at + wd, :]
        for a in range(4):
            rows = slice(192 * a, 192 * a + 192)
            res = lax.dot_general(gp[p, rows, :], wo, nt, preferred_element_type=F32)
            res += lax.dot_general(gs[p, rows, :], wt, nt, preferred_element_type=F32)
            tps[p][k][a] = res.astype(BF16)
        sa[p, k] = [send(tps[p][k].at[rot(co[p], d)], ras[p][k].at[d - 1], near[p](d)) for d in (1, 3, 2)]

    def stage_b(p, k):
        ax = (p + 1) % 3
        arrive(*sa[p, k])
        ra = ras[p][k]
        res = tps[p][k][co[p]].astype(F32) + ra[0].astype(F32) + ra[1].astype(F32) + ra[2].astype(F32)
        res = res.astype(BF16)
        for a in range(4):
            tbs[p][k][a] = res[48 * a : 48 * a + 48]
        sb[p, k] = [send(tbs[p][k].at[rot(co[ax], d)], rbs[p][k].at[d - 1], near[ax](d)) for d in (1, 3, 2)]

    def window(i):
        return pl.ds(pl.multiple_of(8 * (i + i // 2), 8), 16)

    def stage_c(p, k):
        ax, ay = (p + 1) % 3, (p + 2) % 3
        arrive(*sb[p, k])
        rb = rbs[p][k]
        tcs[p][k][...] = tbs[p][k][co[ax]].astype(F32) + rb[0].astype(F32) + rb[1].astype(F32) + rb[2].astype(F32)
        sc3[p, k] = [
            send(tcs[p][k].at[window(rot(co[ay], d))], rcs[p][k].at[d - 1], near[ay](d)) for d in (1, 3, 2)]

    def stage_d(p, k):
        start, widths = LANES[p]
        at = start + (widths[0] if k else 0)
        arrive(*sc3[p, k])
        rc = rcs[p][k]
        fin[:, at : at + widths[k]] = tcs[p][k][window(co[(p + 2) % 3]), :] + rc[0] + rc[1] + rc[2]

    heads = []
    for k in range(2):
        for p in range(3):
            if k == 0:
                arrive(gsend[p])
            stage_a(p, k)
    for n in range(4):
        heads.append(head_part(n))
    for p in range(3):
        stage_b(p, 0)
    for n in range(4, 8):
        heads.append(head_part(n))
    for p in range(3):
        stage_c(p, 0)
    for p in range(3):
        stage_b(p, 1)
    for n in range(8, 10):
        heads.append(head_part(n))
    for p in range(3):
        stage_d(p, 0)
    for p in range(3):
        stage_c(p, 1)
    for p in range(3):
        stage_d(p, 1)
    arrive(send(fin, fs, sib))
    for p in range(3):
        start, widths = LANES[p]
        wd = widths[0] + widths[1]
        odd = lax.rem(co[(p + 2) % 3], 2)
        cols = slice(start, start + wd)
        mine, theirs = fin[:, cols], fs[:, cols]

        def rows_of(v):
            even_rows = jnp.where(c == 0, v[0:6], v[6:12])
            odd_rows = jnp.where(c == 0, v[4:10], v[10:16])
            return jnp.where(odd == 0, even_rows, odd_rows).astype(BF16)

        lo = jnp.where(c == 0, mine, theirs)
        hi = jnp.where(c == 0, theirs, mine)
        gx[:, start : start + wd] = rows_of(lo)
        gx[:, HALF + start : HALF + start + wd] = rows_of(hi)

    for cp in heads:
        cp.wait()
    for cp in sent:
        cp.wait_send()
    whole.wait_send()


def shards(hidden_rows, head_weight, teacher_logits, upstream, block_map, token_order):
    vmem = pl.BlockSpec(memory_space=pltpu.VMEM)
    anyw = pl.BlockSpec(memory_space=pl.ANY)
    probs = pl.pallas_call(
        teacher_kernel,
        out_shape=jax.ShapeDtypeStruct((128, 32, 128), BF16),
        in_specs=[pl.BlockSpec(memory_space=pltpu.SMEM), vmem],
        out_specs=vmem,
        compiler_params=pltpu.CompilerParams(vmem_limit_bytes=32 << 20),
        name="teacher_probs",
    )(block_map, teacher_logits)

    def per_unit(shape, dtype):
        return [pltpu.VMEM(shape(wd), dtype) for _, widths in LANES for wd in widths]

    scratch = [
        pltpu.VMEM((2, 4, 4, 48, HALF), BF16),
        pltpu.VMEM((2, HALF, 640), BF16),
        pltpu.VMEM((HALF, 640), BF16),
        pltpu.VMEM((768, 640), F32),
        pltpu.VMEM((768, 640), BF16),
        pltpu.VMEM((128, 32, 128), BF16),
        pltpu.VMEM((768, 640), BF16),
        pltpu.VMEM((16, 128), F32),
        pltpu.VMEM((8, 16, 128), F32),
        pltpu.VMEM((16, 16, 128), F32),
        pltpu.VMEM((3, 768, 768), BF16),
        pltpu.VMEM((3, 768, 640), BF16),
        pltpu.VMEM((3, 768, 640), BF16),
        pltpu.VMEM((5120, 640), BF16),
        pltpu.VMEM((16, HALF), F32),
        pltpu.VMEM((16, HALF), F32),
        *per_unit(lambda wd: (4, 192, wd), BF16),
        *per_unit(lambda wd: (3, 192, wd), BF16),
        *per_unit(lambda wd: (4, 48, wd), BF16),
        *per_unit(lambda wd: (3, 48, wd), BF16),
        *per_unit(lambda wd: (48, wd), F32),
        *per_unit(lambda wd: (3, 16, wd), F32),
        pltpu.SemaphoreType.DMA((128,)),
        pltpu.SemaphoreType.DMA((128,)),
        pltpu.SemaphoreType.DMA((16,)),
        pltpu.SemaphoreType.DMA,
        pltpu.SemaphoreType.DMA,
    ]
    return pl.pallas_call(
        head_kernel,
        out_shape=(jax.ShapeDtypeStruct((5120, 640), BF16), jax.ShapeDtypeStruct((6, 5120), BF16)),
        in_specs=[anyw, anyw, anyw, vmem, vmem],
        out_specs=(anyw, vmem),
        scratch_shapes=scratch,
        compiler_params=pltpu.CompilerParams(
            collective_id=0, has_side_effects=True, vmem_limit_bytes=62 << 20),
        name="head_backward",
    )(
        hidden_rows.reshape(2, 48, 5120),
        head_weight.reshape(2, HALF, 640),
        probs,
        upstream.reshape(6, 128),
        token_order.astype(F32).reshape(1, 768),
    )


def solution(mesh):
    in_specs = (P("dp", None), P(None, ("dp", "vocab")), P(("dp", "vocab"), None), P(), P(), P())
    out_specs = (P(None, ("dp", "vocab")), P(("dp", "vocab"), None))
    return jax.shard_map(shards, mesh=mesh, in_specs=in_specs, out_specs=out_specs, check_vma=False)
```

time: 882 us -> 132 us (0.15)
  blocking collectives: 492 us -> 0 us
  waiting for transfers between devices: 154 us -> 0 us
  Pallas kernels: 0 us -> 120 us
  starting transfers between devices: 103 us -> 0 us
  local copies, waits for them, and re-layouts: 70.2 us -> 10.4 us
  matrix products: 34.2 us -> 0 us
  between operations: 15 us -> 0.67 us
    unnamed x1 -> x0, blocking collectives: 360 us -> none
    all_gather x1 -> x0, waiting for transfers between devices: 121 us -> none  [shards(): gathered = lax.all_gather(hidden_rows, 'dp', axis=0, tiled=True)]
    pallas_call x0 -> x2, Pallas kernels: none -> 120 us  [the longest x1 113 us: shards(): pl.pallas_call(head_kernel, out_shape=(jax.ShapeDtypeStruct((5120, 640),...]
    unnamed x32 -> x0, starting transfers between devices: 90.9 us -> none
    pmax x1 -> x0, blocking collectives: 68.1 us -> none  [shards(): row_max = lax.pmax(local_max, ('dp', 'vocab'))]
    psum x1 -> x0, blocking collectives: 63.8 us -> none  [shards(): row_total = lax.psum(jnp.sum(shifted, axis=1), ('dp', 'vocab'))]
    unnamed x57 -> x10, local copies, waits for them, and re-layouts: 59.5 us -> 9.82 us
    dot_general x3 -> x0, matrix products: 34.2 us -> none  [the longest x1 12.1 us: shards(): lax.dot_general(picked, head_weight, (((1,), (1,)), ((), ())), preferred_...]
  transfers between devices with their start and end apart: 34 -> 0, of which waited for: 2 -> 0; matrix products, arithmetic and copies ran while one was open for 4% -> 0% of each run, Pallas kernels for 0% -> 0%
where the time goes in v1:
time: 132 us
  Pallas kernels  120 us (91%)
  local copies, waits for them, and re-layouts  10.4 us (8%)
    pallas_call x1, Pallas kernels, shards(): pl.pallas_call(head_kernel, out_shape=(jax.ShapeDtypeStruct((5120, 640),...  113 us
    unnamed x10, local copies, waits for them, and re-layouts  9.82 us
    pallas_call x1, Pallas kernels, shards(): pl.pallas_call(teacher_kernel, out_shape=jax.ShapeDtypeStruct((128, 32, 1...  7.71 us

profile of v1, /device:TPU:1, one launch (start us, length us, event | category | flops | bytes accessed | tf_op | source)
XLA Modules:
  0.0 132.0 jit_solution(17334541271090083269)
XLA Ops:
  0.6 0.7 convert_element_type.3
  1.3 0.6 reshape.19.tok
  1.9 0.0 copy-start.1
  1.9 1.3 copy-done.1
  3.2 0.0 copy-start.2
  3.2 0.7 copy-done.2
  3.9 7.7 %teacher_probs.1.tea = bf16[128,32,128]{2,1,0:T(8,128)(2,1)S(1)} custom-call(s32[32]{0:T(128)S(1)} %copy-done.2, bf16[6,81920]{1,0:T(8,128)(2,1)S(1)} %copy-done.1), custom_call_target="tpu_custom_call" | custom-call | tf_op jit(solution)/shard_map/teacher_probs/pallas_call | solution.py:429
  11.6 0.0 copy-start
  11.6 1.0 copy-done
  12.6 112.5 %head_backward.1 = (bf16[5120,640]{1,0:T(8,128)(2,1)}, bf16[6,5120]{1,0:T(8,128)(2,1)}) custom-call(bf16[2,48,5120]{2,1,0:T(8,128)(2,1)} %bitcast.4, bf16[2,2560,640]{2,1,0:T(8,128)(2,1)} %bitcast.3, bf16[128,32,128]{2,1,0:T(8,128)(2,1)} %copy-done, f32[6,128]{1,0:T(8,128)} %bitcast.5, f32[1,768]{1,0:T(1,128)} %reshape.19.tok), custom_call_target="tpu_custom_call" | custom-call | tf_op jit(solution)/shard_map/head_backward/pallas_call | solution.py:470
  125.1 0.0 copy-start.3
  125.1 6.2 %copy.10 = bf16[5120,640]{1,0:T(8,128)(2,1)} copy(bf16[5120,640]{1,0:T(8,128)(2,1)} %get-tuple-element.4) | data formatting | bytes 13107200
  131.4 0.0 copy-done.3
  131.4 0.6 copy.11
Async XLA Ops:
  1.9 1.3 copy-start.1
  3.2 0.7 copy-start.2
  11.6 1.0 copy-start
  125.1 6.3 %copy-start.3 = (bf16[6,5120]{1,0:T(8,128)(2,1)S(1)}, bf16[6,5120]{1,0:T(8,128)(2,1)}, u32[]{:S(2)}) copy-start(bf16[6,5120]{1,0:T(8,128)(2,1)} %get-tuple-element.5) | copy-start | bytes 184324

commit v2 on v1

--- a/solution.py
+++ b/solution.py
@@ -18,40 +18,13 @@
     return (x * 2 + lax.rem(z, 2), (z // 2) * 8 + y * 2 + c)
 
 
-def teacher_kernel(bmap, t_ref, o_ref):
-    width = 2560
-
-    def top(j, m):
-        cols = pl.ds(pl.multiple_of(j * width, width), width)
-        return jnp.maximum(m, jnp.max(t_ref[:, cols].astype(F32), axis=1, keepdims=True))
-
-    m = lax.fori_loop(0, 32, top, jnp.full((6, 1), -jnp.inf, F32))
-
-    def add(j, s):
-        cols = pl.ds(pl.multiple_of(j * width, width), width)
-        return s + jnp.sum(jnp.exp(t_ref[:, cols].astype(F32) - m), axis=1, keepdims=True)
-
-    s = lax.fori_loop(0, 32, add, jnp.zeros((6, 1), F32))
-    pad = jnp.zeros((2, 128), F32)
-
-    def block(j, carry):
-        cols = pl.ds(pl.multiple_of(bmap[j] * width, width), width)
-        p = jnp.exp(t_ref[:, cols].astype(F32) - m) / s
-        for k in range(4):
-            rows = [p[:, 640 * k + 128 * i : 640 * k + 128 * i + 128] for i in range(5)]
-            o_ref[4 * j + k] = jnp.concatenate(rows + [pad], axis=0).astype(BF16)
-        return carry
-
-    lax.fori_loop(0, 32, block, 0)
-
-
 def head_kernel(
-    hid, w, tea, ups, tok, gh, gx,
-    hb, wb, ws, acc, qb, rt, g, st0, st1, st2, perm, gp, gs, ghb, fin, fs,
+    hid, w, tea, bmap, ups, tok, gh, gx,
+    hb, wb, ws, acc, qb, rt, tv, mt, g, st0, st1, st2, perm, gp, gs, ghb, fin, fs,
     t00, t01, t10, t11, t20, t21, a00, a01, a10, a11, a20, a21,
     u00, u01, u10, u11, u20, u21, b00, b01, b10, b11, b20, b21,
     v00, v01, v10, v11, v20, v21, c00, c01, c10, c11, c20, c21,
-    ss, rs, ls, tss, trs,
+    ss, rs, ls, tss, trs, hx, hy, hc,
 ):
     tps = ((t00, t01), (t10, t11), (t20, t21))
     ras = ((a00, a01), (a10, a11), (a20, a21))
@@ -115,18 +88,20 @@
     other.start()
     wcopy = pltpu.make_async_copy(w, wb, ls.at[2])
     wcopy.start()
-    tcopy = pltpu.make_async_copy(tea.at[me], rt.at[me], ls.at[3])
-    tcopy.start()
+    def fetch(j, carry):
+        cols = pl.ds(pl.multiple_of(j * HALF, 128), HALF)
+        pltpu.make_async_copy(tea.at[:, cols], tv.at[j], ls.at[3]).start()
+        return carry
+
+    lax.fori_loop(0, 32, fetch, 0)
+    tcopy = pltpu.make_async_copy(tv, tv, ls.at[3])
 
     bar = pltpu.get_barrier_semaphore()
 
-    def greet(i, carry):
-        t = lax.rem(me + i, 128)
-        pl.semaphore_signal(bar, inc=1, device_id=(t // 16, lax.rem(t, 16)), device_id_type=MESH)
-        return carry
-
-    lax.fori_loop(1, 128, greet, 0)
-    pl.semaphore_wait(bar, 127)
+    peers = [f(d) for f in (xn, yn, zn) for d in (1, 3, 2)] + [sib]
+    for to in peers:
+        pl.semaphore_signal(bar, inc=1, device_id=to, device_id_type=MESH)
+    pl.semaphore_wait(bar, len(peers))
     for cp in own:
         cp.wait()
 
@@ -140,36 +115,92 @@
         return send(ref, ref, to)
 
     xs, zs = pl.ds(0, XW), pl.ds(Z0, ZW)
-    px = (same(hb.at[c, x, q0, :, xs], zn(1)), same(hb.at[c, x, q0 + 1, :, xs], zn(3)))
-    py = (same(hb.at[c, x, q0, :, ysl(y)], zn(1)), same(hb.at[c, x, q0 + 1, :, ysl(y)], zn(3)))
-    z1 = [same(hb.at[c, x, zq(z), :, zs], xn(d)) for d in (1, 3, 2)]
-    y1 = [same(hb.at[c, x, pl.ds(q0, 2), :, ysl(y)], xn(d)) for d in (1, 3, 2)]
-    x1 = [same(hb.at[c, x, pl.ds(q0, 2), :, xs], xn(d)) for d in (1, 3, 2)]
-    wx = send(w.at[o], ws, sib)
-    arrive(*py)
-    y2 = [same(hb.at[c, x, pl.ds(qo, 2), :, ysl(y)], xn(d)) for d in (1, 3, 2)]
-    arrive(*px)
-    x2 = [same(hb.at[c, x, pl.ds(qo, 2), :, xs], xn(d)) for d in (1, 3, 2)]
-    dx0 = same(hb.at[c, x, pl.ds(qo, 2), :, xs], sib)
-    arrive(*z1)
-    z2 = [same(hb.at[c, :, zq(z), :, zs], zn(d)) for d in (1, 3, 2)]
-    dz0 = same(hb.at[c, :, zq(z), :, zs], sib)
-    arrive(*y1)
-    arrive(*y2)
-    y3 = [same(hb.at[c, :, :, :, ysl(y)], yn(d)) for d in (1, 3, 2)]
-    dy0 = same(hb.at[c, :, :, :, ysl(y)], sib)
-
-    def give(i, carry):
-        t = lax.rem(me + i, 128)
-        pltpu.make_async_remote_copy(
-            src_ref=tea.at[t], dst_ref=rt.at[me], send_sem=tss, recv_sem=trs,
-            device_id=(t // 16, lax.rem(t, 16)), device_id_type=MESH,
-        ).start()
-        return carry
-
-    lax.fori_loop(1, 128, give, 0)
-
-    acc[...] = jnp.zeros_like(acc)
+    za, zb = pl.ds(Z0, ZW // 2), pl.ds(Z0 + ZW // 2, ZW // 2)
+
+    def greet(sem, to):
+        for dev in to:
+            pl.semaphore_signal(sem, inc=1, device_id=dev, device_id_type=MESH)
+
+    def fold(v, op):
+        r = v[:, 0:128]
+        for n in range(1, 20):
+            r = op(r, v[:, 128 * n : 128 * n + 128])
+        return r
+
+    def tea_cols(j):
+        return tv[j].astype(F32)
+
+    def tea_max():
+        top = lax.fori_loop(
+            0, 32, lambda j, m: jnp.maximum(m, fold(tea_cols(j), jnp.maximum)), jnp.full((6, 128), -jnp.inf, F32))
+        return jnp.max(top, axis=1, keepdims=True)
+
+    def tea_sum(m):
+        tot = lax.fori_loop(
+            0, 32, lambda j, s: s + fold(jnp.exp(tea_cols(j) - m), jnp.add), jnp.zeros((6, 128), F32))
+        return jnp.sum(tot, axis=1, keepdims=True)
+
+    def tea_write(m, s, lo, hi):
+        inv = 1.0 / s
+        pad = jnp.zeros((2, 128), F32)
+
+        def block(j, carry):
+            p = jnp.exp(tea_cols(bmap[j]) - m) * inv
+            for n in range(4):
+                rows = [p[:, 640 * n + 128 * i : 640 * n + 128 * i + 128] for i in range(5)]
+                mt[4 * j + n] = jnp.concatenate(rows + [pad], axis=0).astype(BF16)
+            return carry
+
+        lax.fori_loop(lo, hi, block, 0)
+
+    def give(lo, hi):
+        def one(i, carry):
+            t = lax.rem(me + i, 128)
+            pltpu.make_async_remote_copy(
+                src_ref=mt.at[t], dst_ref=rt.at[me], send_sem=tss, recv_sem=trs,
+                device_id=(lax.div(t, 16), lax.rem(t, 16)), device_id_type=MESH,
+            ).start()
+            return carry
+
+        lax.fori_loop(lo, hi, one, 0)
+
+    class Ring:
+        def __init__(self, near, at, part, half, own_to_sib=True):
+            self.near, self.at, self.part, self.half, self.own_to_sib = near, at, part, half, own_to_sib
+
+        def start(self):
+            ref = self.part(self.at)
+            self.right, self.left = same(ref, self.near(1)), same(ref, self.near(3))
+            self.own = same(ref, sib) if self.own_to_sib else None
+
+        def forward(self):
+            before, after = rot(self.at, 3), rot(self.at, 1)
+            arrive(self.right)
+            self.far = [same(self.half(before, 0), self.near(1))]
+            arrive(self.left)
+            self.far.append(same(self.half(after, 1), self.near(3)))
+            self.sides = [same(self.part(before), sib), same(self.part(after), sib)]
+
+        def finish(self):
+            arrive(*self.far)
+            self.end = same(self.part(rot(self.at, 2)), sib)
+
+    def xring(q, own_to_sib):
+        return Ring(
+            xn, x, lambda v: hb.at[c, v, pl.ds(q, 2), :, xs], lambda v, i: hb.at[c, v, q + i, :, xs], own_to_sib)
+
+    def yring(q):
+        return Ring(
+            yn, y, lambda v: hb.at[c, :, pl.ds(q, 2), :, ysl(v)],
+            lambda v, i: hb.at[c, pl.ds(2 * i, 2), pl.ds(q, 2), :, ysl(v)])
+
+    def zring(cols):
+        return Ring(
+            zn, z, lambda v: hb.at[c, :, zq(v), :, cols], lambda v, i: hb.at[c, pl.ds(2 * i, 2), zq(v), :, cols])
+
+    xra, xrb = xring(q0, False), xring(qo, True)
+    yra, yrb = yring(q0), yring(qo)
+    zra, zrb = zring(za), zring(zb)
 
     def mul_x(h, xx):
         lhs = hb[h, xx, :, :, xs].reshape(192, XW)
@@ -188,7 +219,7 @@
             rows = pl.ds(pl.multiple_of(192 * xx + 48 * q, 16), 48)
             acc[rows, :] += res[48 * xx : 48 * xx + 48]
 
-    for p in range(3):
+    def make_perm(p):
         for a in range(6):
             i = lax.broadcasted_iota(jnp.int32, (128, 1), 0) + 128 * a
             n = (i * 43691) >> 19
@@ -197,45 +228,100 @@
             first, second, third = n >> 4, (n >> 2) & 3, n & 3
             rx, ry, rz = ((first, second, third), (third, first, second), (second, third, first))[p]
             row = 6 * ((rx * 2 + (rz & 1)) * 16 + (rz >> 1) * 8 + ry * 2 + core) + k - 6 * core
+            lane = lax.broadcasted_iota(jnp.int32, (128, 128), 1)
+            token = jnp.zeros((128, 128), F32)
+            for b in range(6):
+                token += jnp.where(lane == row - 128 * b, tok[b : b + 1, :].astype(F32), 0.0)
+            token = jnp.sum(token, axis=1, keepdims=True)
             col = lax.broadcasted_iota(jnp.int32, (128, 768), 1)
-            token = jnp.sum(jnp.where(col == row, tok[...], 0.0), axis=1, keepdims=True)
             perm[p, 128 * a : 128 * a + 128, :] = jnp.where(col.astype(F32) == token, 1.0, 0.0).astype(BF16)
 
+    own2, two = pl.ds(q0, 2), pl.ds(qo, 2)
+    y1 = [same(hb.at[c, x, own2, :, ysl(y)], xn(d)) for d in (1, 3, 2)]
+    py = (same(hb.at[c, x, q0, :, ysl(y)], zn(1)), same(hb.at[c, x, q0 + 1, :, ysl(y)], zn(3)))
+    za1 = [same(hb.at[c, x, zq(z), :, za], xn(d)) for d in (1, 3, 2)]
+    px = (same(hb.at[c, x, q0, :, xs], zn(1)), same(hb.at[c, x, q0 + 1, :, xs], zn(3)))
+    greet(hx, [xn(d) for d in (1, 3, 2)])
+    wx = send(w.at[o], ws, sib)
+    tcopy.wait()
+    tm = tea_max()
+    arrive(*py)
+    y2 = [same(hb.at[c, x, two, :, ysl(y)], xn(d)) for d in (1, 3, 2)]
+    zb1 = [same(hb.at[c, x, zq(z), :, zb], xn(d)) for d in (1, 3, 2)]
+    pl.semaphore_wait(hx, 3)
+    greet(hy, [yn(d) for d in (1, 3, 2)])
+    arrive(*y1)
+    yra.start()
+    arrive(*za1)
+    zra.start()
+    xra.start()
+    ts = tea_sum(tm)
+    pl.semaphore_wait(hy, 3)
+    greet(hc, [sib])
+    arrive(*px)
+    xrb.start()
+    tea_write(tm, ts, 0, 16)
+    arrive(*y2)
+    yrb.start()
+    arrive(*zb1)
+    zrb.start()
+    tea_write(tm, ts, 16, 32)
+    pl.semaphore_wait(hc, 1)
+    rt[me] = mt[me]
+    yra.forward()
+    give(1, 17)
+    zra.forward()
+    give(17, 33)
+    xra.forward()
     wcopy.wait()
+    acc[...] = jnp.zeros_like(acc)
     mul_x(c, x)
+    give(33, 49)
     mul_z(c, z)
+    xrb.forward()
+    give(49, 65)
+    yrb.forward()
+    give(65, 81)
+    zrb.forward()
+    give(81, 97)
     mul_y(c, y)
+    give(97, 113)
     other.wait()
-    arrive(dx0)
+    arrive(xrb.own)
     mul_x(o, x)
-    arrive(dz0)
+    give(113, 128)
+    arrive(zra.own, zrb.own)
     mul_z(o, z)
-    arrive(dy0)
+    arrive(yra.own, yrb.own)
     mul_y(o, y)
-    dxs, dzs, dys = [], [], []
-    for i, d in enumerate((3, 1, 2)):
-        arrive(x1[i], x2[i])
-        dxs.append(same(hb.at[c, rot(x, d), :, :, xs], sib))
+    for p in range(3):
+        make_perm(p)
+    for d in (3, 1):
         mul_x(c, rot(x, d))
-    for i, d in enumerate((3, 1, 2)):
-        arrive(z2[i])
-        dzs.append(same(hb.at[c, :, zq(rot(z, d)), :, zs], sib))
-        arrive(y3[i])
-        dys.append(same(hb.at[c, :, :, :, ysl(rot(y, d))], sib))
-        arrive(dxs[i])
+        mul_y(c, rot(y, d))
+        mul_z(c, rot(z, d))
+    xra.finish()
+    xrb.finish()
+    mul_x(c, rot(x, 2))
+    yra.finish()
+    zra.finish()
+    for i, d in enumerate((3, 1)):
+        arrive(xra.sides[i], xrb.sides[i])
         mul_x(o, rot(x, d))
-        mul_z(c, rot(z, d))
-        mul_y(c, rot(y, d))
-        if i > 0:
-            e = (3, 1, 2)[i - 1]
-            arrive(dzs[i - 1])
-            mul_z(o, rot(z, e))
-            arrive(dys[i - 1])
-            mul_y(o, rot(y, e))
-    arrive(dzs[2])
+        arrive(yra.sides[i], yrb.sides[i])
+        mul_y(o, rot(y, d))
+        arrive(zra.sides[i], zrb.sides[i])
+        mul_z(o, rot(z, d))
+    yrb.finish()
+    zrb.finish()
+    mul_y(c, rot(y, 2))
+    mul_z(c, rot(z, 2))
+    arrive(xra.end, xrb.end)
+    mul_x(o, rot(x, 2))
+    arrive(yra.end, yrb.end)
+    mul_y(o, rot(y, 2))
+    arrive(zra.end, zrb.end)
     mul_z(o, rot(z, 2))
-    arrive(dys[2])
-    mul_y(o, rot(y, 2))
 
     eye = lax.broadcasted_iota(jnp.int32, (128, 128), 0) == lax.broadcasted_iota(jnp.int32, (128, 128), 1)
     st0[...] = jnp.zeros_like(st0)
@@ -280,9 +366,8 @@
             if d + e > 0:
                 cps.append(send(st2.at[0], st2.at[4 * d + e], device(x, rot(y, d), rot(z, e), c)))
 
-    tcopy.wait()
     whole = pltpu.make_async_remote_copy(
-        src_ref=tea.at[pl.ds(0, 127)], dst_ref=rt.at[pl.ds(0, 127)], send_sem=tss, recv_sem=trs,
+        src_ref=mt.at[pl.ds(0, 127)], dst_ref=rt.at[pl.ds(0, 127)], send_sem=tss, recv_sem=trs,
         device_id=sib, device_id_type=MESH,
     )
     whole.wait_recv()
@@ -317,7 +402,7 @@
             rows = slice(256 * a, 256 * a + 256)
             gp[p, rows, :] = jnp.dot(perm[p, rows, :], g[...], preferred_element_type=F32).astype(BF16)
         gsend.append(send(gp.at[p], gs.at[p], sib))
-    wx.wait_recv()
+    arrive(wx)
 
     co = (x, y, z)
     near = (xn, yn, zn)
@@ -339,18 +424,32 @@
         at = start + (widths[0] if k else 0)
         wo = wb[c, at : at + wd, :]
         wt = ws[at : at + wd, :]
-        for a in range(4):
-            rows = slice(192 * a, 192 * a + 192)
+        tp, ra, v = tps[p][k], ras[p][k], co[p]
+        on, back = ((1, 3), (3, 1))[k]
+        sa[p, k] = []
+        for d in (2, back, on, 0):
+            a = rot(v, d)
+            rows = pl.ds(pl.multiple_of(192 * a, 64), 192)
             res = lax.dot_general(gp[p, rows, :], wo, nt, preferred_element_type=F32)
             res += lax.dot_general(gs[p, rows, :], wt, nt, preferred_element_type=F32)
-            tps[p][k][a] = res.astype(BF16)
-        sa[p, k] = [send(tps[p][k].at[rot(co[p], d)], ras[p][k].at[d - 1], near[p](d)) for d in (1, 3, 2)]
+            tp[a] = res.astype(BF16)
+            if d == 2:
+                sa[p, k].append(send(tp.at[a], ra.at[2], near[p](on)))
+            if d == back:
+                sa[p, k].append(send(tp.at[a], ra.at[0], near[p](back)))
+
+    def pass_a(p, k):
+        tp, ra, on = tps[p][k], ras[p][k], (1, 3)[k]
+        arrive(sa[p, k][0])
+        a = rot(co[p], on)
+        tp[a] = (tp[a].astype(F32) + ra[2].astype(F32)).astype(BF16)
+        sa[p, k].append(send(tp.at[a], ra.at[1], near[p](on)))
 
     def stage_b(p, k):
         ax = (p + 1) % 3
-        arrive(*sa[p, k])
+        arrive(*sa[p, k][1:])
         ra = ras[p][k]
-        res = tps[p][k][co[p]].astype(F32) + ra[0].astype(F32) + ra[1].astype(F32) + ra[2].astype(F32)
+        res = tps[p][k][co[p]].astype(F32) + ra[0].astype(F32) + ra[1].astype(F32)
         res = res.astype(BF16)
         for a in range(4):
             tbs[p][k][a] = res[48 * a : 48 * a + 48]
@@ -375,21 +474,26 @@
         fin[:, at : at + widths[k]] = tcs[p][k][window(co[(p + 2) % 3]), :] + rc[0] + rc[1] + rc[2]
 
     heads = []
-    for k in range(2):
-        for p in range(3):
-            if k == 0:
-                arrive(gsend[p])
-            stage_a(p, k)
-    for n in range(4):
+    for p in range(3):
+        arrive(gsend[p])
+        stage_a(p, 0)
+    for p in range(3):
+        stage_a(p, 1)
+        pass_a(p, 0)
+    for n in range(2):
         heads.append(head_part(n))
     for p in range(3):
+        pass_a(p, 1)
+    for n in range(2, 5):
+        heads.append(head_part(n))
+    for p in range(3):
         stage_b(p, 0)
-    for n in range(4, 8):
+    for n in range(5, 8):
         heads.append(head_part(n))
     for p in range(3):
+        stage_b(p, 1)
+    for p in range(3):
         stage_c(p, 0)
-    for p in range(3):
-        stage_b(p, 1)
     for n in range(8, 10):
         heads.append(head_part(n))
     for p in range(3):
@@ -426,15 +530,6 @@
 def shards(hidden_rows, head_weight, teacher_logits, upstream, block_map, token_order):
     vmem = pl.BlockSpec(memory_space=pltpu.VMEM)
     anyw = pl.BlockSpec(memory_space=pl.ANY)
-    probs = pl.pallas_call(
-        teacher_kernel,
-        out_shape=jax.ShapeDtypeStruct((128, 32, 128), BF16),
-        in_specs=[pl.BlockSpec(memory_space=pltpu.SMEM), vmem],
-        out_specs=vmem,
-        compiler_params=pltpu.CompilerParams(vmem_limit_bytes=32 << 20),
-        name="teacher_probs",
-    )(block_map, teacher_logits)
-
     def per_unit(shape, dtype):
         return [pltpu.VMEM(shape(wd), dtype) for _, widths in LANES for wd in widths]
 
@@ -444,6 +539,8 @@
         pltpu.VMEM((HALF, 640), BF16),
         pltpu.VMEM((768, 640), F32),
         pltpu.VMEM((768, 640), BF16),
+        pltpu.VMEM((128, 32, 128), BF16),
+        pltpu.VMEM((32, 6, HALF), BF16),
         pltpu.VMEM((128, 32, 128), BF16),
         pltpu.VMEM((768, 640), BF16),
         pltpu.VMEM((16, 128), F32),
@@ -461,16 +558,19 @@
         *per_unit(lambda wd: (3, 48, wd), BF16),
         *per_unit(lambda wd: (48, wd), F32),
         *per_unit(lambda wd: (3, 16, wd), F32),
-        pltpu.SemaphoreType.DMA((128,)),
-        pltpu.SemaphoreType.DMA((128,)),
+        pltpu.SemaphoreType.DMA((160,)),
+        pltpu.SemaphoreType.DMA((160,)),
         pltpu.SemaphoreType.DMA((16,)),
         pltpu.SemaphoreType.DMA,
         pltpu.SemaphoreType.DMA,
+        pltpu.SemaphoreType.REGULAR,
+        pltpu.SemaphoreType.REGULAR,
+        pltpu.SemaphoreType.REGULAR,
     ]
     return pl.pallas_call(
         head_kernel,
         out_shape=(jax.ShapeDtypeStruct((5120, 640), BF16), jax.ShapeDtypeStruct((6, 5120), BF16)),
-        in_specs=[anyw, anyw, anyw, vmem, vmem],
+        in_specs=[anyw, anyw, anyw, pl.BlockSpec(memory_space=pltpu.SMEM), vmem, vmem],
         out_specs=(anyw, vmem),
         scratch_shapes=scratch,
         compiler_params=pltpu.CompilerParams(
@@ -479,9 +579,10 @@
     )(
         hidden_rows.reshape(2, 48, 5120),
         head_weight.reshape(2, HALF, 640),
-        probs,
+        teacher_logits,
+        block_map,
         upstream.reshape(6, 128),
-        token_order.astype(F32).reshape(1, 768),
+        token_order.reshape(6, 128),
     )
 
 

time: 132 us -> 108 us (0.82)
  Pallas kernels: 120 us -> 100 us
  local copies, waits for them, and re-layouts: 10.4 us -> 6.88 us
    pallas_call x1, Pallas kernels: 113 us -> 100 us  [shards(): pl.pallas_call(head_kernel, out_shape=(jax.ShapeDtypeStruct((5120, 640),...]
    pallas_call x1 -> x0, Pallas kernels: 7.71 us -> none  [shards(): pl.pallas_call(teacher_kernel, out_shape=jax.ShapeDtypeStruct((128, 32, 1...]
    unnamed x10 -> x4, local copies, waits for them, and re-layouts: 9.82 us -> 6.88 us
where the time goes in v2:
time: 108 us; the launch traced here: 107 us
  Pallas kernels  100 us (93%)
  local copies, waits for them, and re-layouts  6.88 us (6%)
    pallas_call x1, Pallas kernels, shards(): pl.pallas_call(head_kernel, out_shape=(jax.ShapeDtypeStruct((5120, 640),...  100 us
    unnamed x4, local copies, waits for them, and re-layouts  6.88 us

profile of v2, /device:TPU:1, one launch (start us, length us, event | category | flops | bytes accessed | tf_op | source)
XLA Modules:
  0.0 107.5 jit_solution(17567284358178651432)
XLA Ops:
  0.6 100.0 %head_backward.1 = (bf16[5120,640]{1,0:T(8,128)(2,1)}, bf16[6,5120]{1,0:T(8,128)(2,1)}) custom-call(bf16[2,48,5120]{2,1,0:T(8,128)(2,1)} %bitcast.5, bf16[2,2560,640]{2,1,0:T(8,128)(2,1)} %bitcast.4, bf16[6,81920]{1,0:T(8,128)(2,1)} %tea.1, s32[32]{0:T(128)} %bmap.1, f32[6,128]{1,0:T(8,128)} %bitcast.6, s32[6,128]{1,0:T(8,128)} %bitcast.7), custom_call_target="tpu_custom_call" | custom-call | tf_op jit(solution)/shard_map/head_backward/pallas_call | solution.py:570
  100.6 0.0 copy-start
  100.6 6.2 %copy.10 = bf16[5120,640]{1,0:T(8,128)(2,1)} copy(bf16[5120,640]{1,0:T(8,128)(2,1)} %get-tuple-element.4) | data formatting | bytes 13107200
  106.8 0.0 copy-done
  106.8 0.6 copy.11
Async XLA Ops:
  100.6 6.3 %copy-start = (bf16[6,5120]{1,0:T(8,128)(2,1)S(1)}, bf16[6,5120]{1,0:T(8,128)(2,1)}, u32[]{:S(2)}) copy-start(bf16[6,5120]{1,0:T(8,128)(2,1)} %get-tuple-element.5) | copy-start | bytes 184324

commit v3 on v2

--- a/solution.py
+++ b/solution.py
@@ -11,7 +11,8 @@
 HALF = 2560
 XW, YW, ZW = 512, 256, 1024
 Y0, Z0 = 512, 1536
-LANES = ((0, (512, 384)), (896, (512, 384)), (1792, (384, 384)))
+UNITS = (((0, 512), (512, 256)), ((768, 512), (1280, 256)), ((1536, 512), (2048, 512)))
+AXES = ((0, 1, 2), (1, 0, 2), (2, 0, 1))
 
 
 def device(x, y, z, c):
@@ -20,11 +21,11 @@
 
 def head_kernel(
     hid, w, tea, bmap, ups, tok, gh, gx,
-    hb, wb, ws, acc, qb, rt, tv, mt, g, st0, st1, st2, perm, gp, gs, ghb, fin, fs,
+    hb, wb, wc, acc, qb, rr, rt, tv, mt, g, st0, st1, st2, perm, gc, ghb, fin, fs,
     t00, t01, t10, t11, t20, t21, a00, a01, a10, a11, a20, a21,
     u00, u01, u10, u11, u20, u21, b00, b01, b10, b11, b20, b21,
     v00, v01, v10, v11, v20, v21, c00, c01, c10, c11, c20, c21,
-    ss, rs, ls, tss, trs, hx, hy, hc,
+    ss, rs, ls, tss, trs, hx, hy,
 ):
     tps = ((t00, t01), (t10, t11), (t20, t21))
     ras = ((a00, a01), (a10, a11), (a20, a21))
@@ -69,6 +70,11 @@
         for cp in cps:
             cp.wait_recv()
 
+    bar = pltpu.get_barrier_semaphore()
+
+    peers = [f(d) for f in (xn, yn, zn) for d in (1, 3, 2)] + [sib]
+    for to in peers:
+        pl.semaphore_signal(bar, inc=1, device_id=to, device_id_type=MESH)
     q0, qo = 2 * zl, 2 * (1 - zl)
     mine = pl.multiple_of(HALF * c, 128)
     own = (
@@ -82,25 +88,6 @@
     )
     for cp in own:
         cp.start()
-    other = pltpu.make_async_copy(
-        hid.at[:, :, pl.ds(pl.multiple_of(HALF * o, 128), XW)],
-        hb.at[o, x, pl.ds(q0, 2), :, pl.ds(0, XW)], ls.at[1])
-    other.start()
-    wcopy = pltpu.make_async_copy(w, wb, ls.at[2])
-    wcopy.start()
-    def fetch(j, carry):
-        cols = pl.ds(pl.multiple_of(j * HALF, 128), HALF)
-        pltpu.make_async_copy(tea.at[:, cols], tv.at[j], ls.at[3]).start()
-        return carry
-
-    lax.fori_loop(0, 32, fetch, 0)
-    tcopy = pltpu.make_async_copy(tv, tv, ls.at[3])
-
-    bar = pltpu.get_barrier_semaphore()
-
-    peers = [f(d) for f in (xn, yn, zn) for d in (1, 3, 2)] + [sib]
-    for to in peers:
-        pl.semaphore_signal(bar, inc=1, device_id=to, device_id_type=MESH)
     pl.semaphore_wait(bar, len(peers))
     for cp in own:
         cp.wait()
@@ -148,17 +135,19 @@
             p = jnp.exp(tea_cols(bmap[j]) - m) * inv
             for n in range(4):
                 rows = [p[:, 640 * n + 128 * i : 640 * n + 128 * i + 128] for i in range(5)]
-                mt[4 * j + n] = jnp.concatenate(rows + [pad], axis=0).astype(BF16)
+                mt[2 * j + n // 2, n % 2] = jnp.concatenate(rows + [pad], axis=0).astype(BF16)
             return carry
 
         lax.fori_loop(lo, hi, block, 0)
+
+    chip = lax.div(me, 2)
 
     def give(lo, hi):
         def one(i, carry):
-            t = lax.rem(me + i, 128)
+            t = lax.rem(chip + i, 64)
             pltpu.make_async_remote_copy(
-                src_ref=mt.at[t], dst_ref=rt.at[me], send_sem=tss, recv_sem=trs,
-                device_id=(lax.div(t, 16), lax.rem(t, 16)), device_id_type=MESH,
+                src_ref=mt.at[t], dst_ref=rr.at[chip], send_sem=tss, recv_sem=trs,
+                device_id=(lax.div(t, 8), 2 * lax.rem(t, 8) + c), device_id_type=MESH,
             ).start()
             return carry
 
@@ -226,7 +215,7 @@
             k = i - 12 * n
             core = jnp.where(k >= 6, 1, 0)
             first, second, third = n >> 4, (n >> 2) & 3, n & 3
-            rx, ry, rz = ((first, second, third), (third, first, second), (second, third, first))[p]
+            rx, ry, rz = ((first, second, third), (second, third, first))[p]
             row = 6 * ((rx * 2 + (rz & 1)) * 16 + (rz >> 1) * 8 + ry * 2 + core) + k - 6 * core
             lane = lax.broadcasted_iota(jnp.int32, (128, 128), 1)
             token = jnp.zeros((128, 128), F32)
@@ -240,14 +229,29 @@
     y1 = [same(hb.at[c, x, own2, :, ysl(y)], xn(d)) for d in (1, 3, 2)]
     py = (same(hb.at[c, x, q0, :, ysl(y)], zn(1)), same(hb.at[c, x, q0 + 1, :, ysl(y)], zn(3)))
     za1 = [same(hb.at[c, x, zq(z), :, za], xn(d)) for d in (1, 3, 2)]
+    zb1 = [same(hb.at[c, x, zq(z), :, zb], xn(d)) for d in (1, 3, 2)]
     px = (same(hb.at[c, x, q0, :, xs], zn(1)), same(hb.at[c, x, q0 + 1, :, xs], zn(3)))
     greet(hx, [xn(d) for d in (1, 3, 2)])
-    wx = send(w.at[o], ws, sib)
+    def fetch(j, carry):
+        cols = pl.ds(pl.multiple_of(j * HALF, 128), HALF)
+        pltpu.make_async_copy(tea.at[:, cols], tv.at[j], ls.at[3]).start()
+        return carry
+
+    lax.fori_loop(0, 32, fetch, 0)
+    tcopy = pltpu.make_async_copy(tv, tv, ls.at[3])
+    other = pltpu.make_async_copy(
+        hid.at[:, :, pl.ds(pl.multiple_of(HALF * o, 128), XW)],
+        hb.at[o, x, pl.ds(q0, 2), :, pl.ds(0, XW)], ls.at[1])
+    other.start()
+    wcopy = pltpu.make_async_copy(w, wb, ls.at[2])
+    wcopy.start()
+    w2copy = pltpu.make_async_copy(w.at[c], wc.at[:, pl.ds(0, 640)], ls.at[16])
+    w2copy.start()
+    wx = send(w.at[o], wc.at[:, pl.ds(640, 640)], sib)
     tcopy.wait()
     tm = tea_max()
     arrive(*py)
     y2 = [same(hb.at[c, x, two, :, ysl(y)], xn(d)) for d in (1, 3, 2)]
-    zb1 = [same(hb.at[c, x, zq(z), :, zb], xn(d)) for d in (1, 3, 2)]
     pl.semaphore_wait(hx, 3)
     greet(hy, [yn(d) for d in (1, 3, 2)])
     arrive(*y1)
@@ -257,7 +261,6 @@
     xra.start()
     ts = tea_sum(tm)
     pl.semaphore_wait(hy, 3)
-    greet(hc, [sib])
     arrive(*px)
     xrb.start()
     tea_write(tm, ts, 0, 16)
@@ -266,36 +269,25 @@
     arrive(*zb1)
     zrb.start()
     tea_write(tm, ts, 16, 32)
-    pl.semaphore_wait(hc, 1)
-    rt[me] = mt[me]
+    rr[chip] = mt[chip]
     yra.forward()
-    give(1, 17)
     zra.forward()
-    give(17, 33)
     xra.forward()
     wcopy.wait()
     acc[...] = jnp.zeros_like(acc)
     mul_x(c, x)
-    give(33, 49)
     mul_z(c, z)
     xrb.forward()
-    give(49, 65)
     yrb.forward()
-    give(65, 81)
     zrb.forward()
-    give(81, 97)
     mul_y(c, y)
-    give(97, 113)
     other.wait()
     arrive(xrb.own)
     mul_x(o, x)
-    give(113, 128)
     arrive(zra.own, zrb.own)
     mul_z(o, z)
     arrive(yra.own, yrb.own)
     mul_y(o, y)
-    for p in range(3):
-        make_perm(p)
     for d in (3, 1):
         mul_x(c, rot(x, d))
         mul_y(c, rot(y, d))
@@ -314,6 +306,7 @@
         mul_z(o, rot(z, d))
     yrb.finish()
     zrb.finish()
+    give(1, 64)
     mul_y(c, rot(y, 2))
     mul_z(c, rot(z, 2))
     arrive(xra.end, xrb.end)
@@ -356,6 +349,7 @@
             if d + e > 0:
                 to = device(rot(x, d), y, z, c if e == 0 else o)
                 cps.append(send(st0, st1.at[2 * d + e], to))
+    make_perm(0)
     arrive(*cps)
     m, s = merge(st0[...], st1, 8)
     st2[0, 0:8, :] = m
@@ -367,10 +361,13 @@
                 cps.append(send(st2.at[0], st2.at[4 * d + e], device(x, rot(y, d), rot(z, e), c)))
 
     whole = pltpu.make_async_remote_copy(
-        src_ref=mt.at[pl.ds(0, 127)], dst_ref=rt.at[pl.ds(0, 127)], send_sem=tss, recv_sem=trs,
+        src_ref=mt.at[pl.ds(0, 63)], dst_ref=rr.at[pl.ds(0, 63)], send_sem=tss, recv_sem=trs,
         device_id=sib, device_id_type=MESH,
     )
     whole.wait_recv()
+    cross = send(rr.at[:, o], rt, sib)
+    make_perm(1)
+    arrive(cross)
     i = lax.broadcasted_iota(jnp.int32, (240, 1), 0)
     j = (i * 1366) >> 16
     k = i - 48 * j
@@ -379,7 +376,9 @@
     pick = jnp.where(lax.broadcasted_iota(jnp.int32, (240, 256), 1) == want, 1.0, 0.0).astype(BF16)
 
     def place(n, carry):
-        src = rt[pl.ds(8 * n, 8)].reshape(256, 128)
+        a, b = rr[pl.ds(4 * n, 4), c], rt[pl.ds(4 * n, 4)]
+        lo, hi = jnp.where(c == 0, a, b), jnp.where(c == 0, b, a)
+        src = jnp.concatenate([v[r] for r in range(4) for v in (lo, hi)], axis=0)
         res = jnp.dot(pick, src, preferred_element_type=F32).astype(BF16)
         for jj in range(5):
             qb[pl.ds(pl.multiple_of(48 * n, 16), 48), 128 * jj : 128 * jj + 128] = res[48 * jj : 48 * jj + 48]
@@ -397,12 +396,13 @@
         g[rows, :] = (acc[rows, :] * sc - uc * qb[rows, :].astype(F32)).astype(BF16)
 
     gsend = []
-    for p in range(3):
+    for p in range(2):
         for a in range(3):
             rows = slice(256 * a, 256 * a + 256)
-            gp[p, rows, :] = jnp.dot(perm[p, rows, :], g[...], preferred_element_type=F32).astype(BF16)
-        gsend.append(send(gp.at[p], gs.at[p], sib))
+            gc[p, rows, 0:640] = jnp.dot(perm[p, rows, :], g[...], preferred_element_type=F32).astype(BF16)
+        gsend.append(send(gc.at[p, :, pl.ds(0, 640)], gc.at[p, :, pl.ds(640, 640)], sib))
     arrive(wx)
+    w2copy.wait()
 
     co = (x, y, z)
     near = (xn, yn, zn)
@@ -418,48 +418,40 @@
         cp.start()
         return cp
 
-    def stage_a(p, k):
-        start, widths = LANES[p]
-        wd = widths[k]
-        at = start + (widths[0] if k else 0)
-        wo = wb[c, at : at + wd, :]
-        wt = ws[at : at + wd, :]
-        tp, ra, v = tps[p][k], ras[p][k], co[p]
+    def partial(p, start, wd):
+        return lax.dot_general(gc[p], wc[start : start + wd, :], nt, preferred_element_type=F32).astype(BF16)
+
+    def stage_a(p, k, res):
+        tp, ra, ax = tps[p][k], ras[p][k], AXES[p][0]
+        for a in range(4):
+            for b in range(4):
+                at = 192 * b + 48 * a if p == 1 else 192 * a + 48 * b
+                tp[a, b] = res[at : at + 48]
+        v, f = co[ax], near[ax]
         on, back = ((1, 3), (3, 1))[k]
-        sa[p, k] = []
-        for d in (2, back, on, 0):
-            a = rot(v, d)
-            rows = pl.ds(pl.multiple_of(192 * a, 64), 192)
-            res = lax.dot_general(gp[p, rows, :], wo, nt, preferred_element_type=F32)
-            res += lax.dot_general(gs[p, rows, :], wt, nt, preferred_element_type=F32)
-            tp[a] = res.astype(BF16)
-            if d == 2:
-                sa[p, k].append(send(tp.at[a], ra.at[2], near[p](on)))
-            if d == back:
-                sa[p, k].append(send(tp.at[a], ra.at[0], near[p](back)))
+        sa[p, k] = [send(tp.at[rot(v, 2)], ra.at[2], f(on)), send(tp.at[rot(v, back)], ra.at[0], f(back))]
 
     def pass_a(p, k):
         tp, ra, on = tps[p][k], ras[p][k], (1, 3)[k]
         arrive(sa[p, k][0])
-        a = rot(co[p], on)
+        ax = AXES[p][0]
+        a = rot(co[ax], on)
         tp[a] = (tp[a].astype(F32) + ra[2].astype(F32)).astype(BF16)
-        sa[p, k].append(send(tp.at[a], ra.at[1], near[p](on)))
+        sa[p, k].append(send(tp.at[a], ra.at[1], near[ax](on)))
 
     def stage_b(p, k):
-        ax = (p + 1) % 3
+        ax = AXES[p][1]
         arrive(*sa[p, k][1:])
         ra = ras[p][k]
-        res = tps[p][k][co[p]].astype(F32) + ra[0].astype(F32) + ra[1].astype(F32)
-        res = res.astype(BF16)
-        for a in range(4):
-            tbs[p][k][a] = res[48 * a : 48 * a + 48]
+        res = tps[p][k][co[AXES[p][0]]].astype(F32) + ra[0].astype(F32) + ra[1].astype(F32)
+        tbs[p][k][...] = res.astype(BF16)
         sb[p, k] = [send(tbs[p][k].at[rot(co[ax], d)], rbs[p][k].at[d - 1], near[ax](d)) for d in (1, 3, 2)]
 
     def window(i):
         return pl.ds(pl.multiple_of(8 * (i + i // 2), 8), 16)
 
     def stage_c(p, k):
-        ax, ay = (p + 1) % 3, (p + 2) % 3
+        ax, ay = AXES[p][1:]
         arrive(*sb[p, k])
         rb = rbs[p][k]
         tcs[p][k][...] = tbs[p][k][co[ax]].astype(F32) + rb[0].astype(F32) + rb[1].astype(F32) + rb[2].astype(F32)
@@ -467,18 +459,18 @@
             send(tcs[p][k].at[window(rot(co[ay], d))], rcs[p][k].at[d - 1], near[ay](d)) for d in (1, 3, 2)]
 
     def stage_d(p, k):
-        start, widths = LANES[p]
-        at = start + (widths[0] if k else 0)
+        start, wd = UNITS[p][k]
         arrive(*sc3[p, k])
         rc = rcs[p][k]
-        fin[:, at : at + widths[k]] = tcs[p][k][window(co[(p + 2) % 3]), :] + rc[0] + rc[1] + rc[2]
+        fin[:, start : start + wd] = tcs[p][k][window(co[AXES[p][2]]), :] + rc[0] + rc[1] + rc[2]
 
     heads = []
-    for p in range(3):
-        arrive(gsend[p])
-        stage_a(p, 0)
-    for p in range(3):
-        stage_a(p, 1)
+    for k in range(2):
+        for p in range(3):
+            if k == 0 and p != 1:
+                arrive(gsend[p // 2])
+            stage_a(p, k, partial(p // 2, *UNITS[p][k]))
+    for p in range(3):
         pass_a(p, 0)
     for n in range(2):
         heads.append(head_part(n))
@@ -504,9 +496,8 @@
         stage_d(p, 1)
     arrive(send(fin, fs, sib))
     for p in range(3):
-        start, widths = LANES[p]
-        wd = widths[0] + widths[1]
-        odd = lax.rem(co[(p + 2) % 3], 2)
+        start, wd = min(u[0] for u in UNITS[p]), sum(u[1] for u in UNITS[p])
+        odd = lax.rem(co[AXES[p][2]], 2)
         cols = slice(start, start + wd)
         mine, theirs = fin[:, cols], fs[:, cols]
 
@@ -531,39 +522,38 @@
     vmem = pl.BlockSpec(memory_space=pltpu.VMEM)
     anyw = pl.BlockSpec(memory_space=pl.ANY)
     def per_unit(shape, dtype):
-        return [pltpu.VMEM(shape(wd), dtype) for _, widths in LANES for wd in widths]
+        return [pltpu.VMEM(shape(wd), dtype) for lane in UNITS for _, wd in lane]
 
     scratch = [
         pltpu.VMEM((2, 4, 4, 48, HALF), BF16),
         pltpu.VMEM((2, HALF, 640), BF16),
-        pltpu.VMEM((HALF, 640), BF16),
+        pltpu.VMEM((HALF, 1280), BF16),
         pltpu.VMEM((768, 640), F32),
         pltpu.VMEM((768, 640), BF16),
-        pltpu.VMEM((128, 32, 128), BF16),
+        pltpu.VMEM((64, 2, 32, 128), BF16),
+        pltpu.VMEM((64, 32, 128), BF16),
         pltpu.VMEM((32, 6, HALF), BF16),
-        pltpu.VMEM((128, 32, 128), BF16),
+        pltpu.VMEM((64, 2, 32, 128), BF16),
         pltpu.VMEM((768, 640), BF16),
         pltpu.VMEM((16, 128), F32),
         pltpu.VMEM((8, 16, 128), F32),
         pltpu.VMEM((16, 16, 128), F32),
-        pltpu.VMEM((3, 768, 768), BF16),
-        pltpu.VMEM((3, 768, 640), BF16),
-        pltpu.VMEM((3, 768, 640), BF16),
+        pltpu.VMEM((2, 768, 768), BF16),
+        pltpu.VMEM((2, 768, 1280), BF16),
         pltpu.VMEM((5120, 640), BF16),
         pltpu.VMEM((16, HALF), F32),
         pltpu.VMEM((16, HALF), F32),
-        *per_unit(lambda wd: (4, 192, wd), BF16),
-        *per_unit(lambda wd: (3, 192, wd), BF16),
+        *per_unit(lambda wd: (4, 4, 48, wd), BF16),
+        *per_unit(lambda wd: (3, 4, 48, wd), BF16),
         *per_unit(lambda wd: (4, 48, wd), BF16),
         *per_unit(lambda wd: (3, 48, wd), BF16),
         *per_unit(lambda wd: (48, wd), F32),
         *per_unit(lambda wd: (3, 16, wd), F32),
         pltpu.SemaphoreType.DMA((160,)),
         pltpu.SemaphoreType.DMA((160,)),
-        pltpu.SemaphoreType.DMA((16,)),
+        pltpu.SemaphoreType.DMA((17,)),
         pltpu.SemaphoreType.DMA,
         pltpu.SemaphoreType.DMA,
-        pltpu.SemaphoreType.REGULAR,
         pltpu.SemaphoreType.REGULAR,
         pltpu.SemaphoreType.REGULAR,
     ]

time: 108 us -> 102 us (0.944)
  Pallas kernels: 100 us -> 94.5 us
    pallas_call x1, Pallas kernels: 100 us -> 94.5 us  [shards(): pl.pallas_call(head_kernel, out_shape=(jax.ShapeDtypeStruct((5120, 640),...]
where the time goes in v3:
time: 102 us
  Pallas kernels  94.5 us (93%)
  local copies, waits for them, and re-layouts  6.88 us (7%)
    pallas_call x1, Pallas kernels, shards(): pl.pallas_call(head_kernel, out_shape=(jax.ShapeDtypeStruct((5120, 640),...  94.5 us
    unnamed x4, local copies, waits for them, and re-layouts  6.88 us

profile of v3, /device:TPU:1, one launch (start us, length us, event | category | flops | bytes accessed | tf_op | source)
XLA Modules:
  0.0 102.1 jit_solution(10521030514530424087)
XLA Ops:
  0.6 94.5 %head_backward.1 = (bf16[5120,640]{1,0:T(8,128)(2,1)}, bf16[6,5120]{1,0:T(8,128)(2,1)}) custom-call(bf16[2,48,5120]{2,1,0:T(8,128)(2,1)} %bitcast.5, bf16[2,2560,640]{2,1,0:T(8,128)(2,1)} %bitcast.4, bf16[6,81920]{1,0:T(8,128)(2,1)} %tea.1, s32[32]{0:T(128)} %bmap.1, f32[6,128]{1,0:T(8,128)} %bitcast.6, s32[6,128]{1,0:T(8,128)} %bitcast.7), custom_call_target="tpu_custom_call" | custom-call | tf_op jit(solution)/shard_map/head_backward/pallas_call | solution.py:560
  95.2 0.0 copy-start
  95.2 6.2 %copy.10 = bf16[5120,640]{1,0:T(8,128)(2,1)} copy(bf16[5120,640]{1,0:T(8,128)(2,1)} %get-tuple-element.4) | data formatting | bytes 13107200
  101.4 0.0 copy-done
  101.4 0.6 copy.11
Async XLA Ops:
  95.2 6.3 %copy-start = (bf16[6,5120]{1,0:T(8,128)(2,1)S(1)}, bf16[6,5120]{1,0:T(8,128)(2,1)}, u32[]{:S(2)}) copy-start(bf16[6,5120]{1,0:T(8,128)(2,1)} %get-tuple-element.5) | copy-start | bytes 184324

commit v4 on v3

--- a/solution.py
+++ b/solution.py
@@ -13,6 +13,19 @@
 Y0, Z0 = 512, 1536
 UNITS = (((0, 512), (512, 256)), ((768, 512), (1280, 256)), ((1536, 512), (2048, 512)))
 AXES = ((0, 1, 2), (1, 0, 2), (2, 0, 1))
+PLAN = (
+    "T20 O T00 T10",
+    "T21 T01 T11 P20",
+    "P00 P10 H H",
+    "P21 P01 P11 H",
+    "H H B20 B00",
+    "B10 H H H",
+    "B21 B01 B11 C20",
+    "C00 C10 H H",
+    "D20 D00 D10 C21",
+    "C01 C11 D21 D01",
+    "D11",
+)
 
 
 def device(x, y, z, c):
@@ -22,17 +35,15 @@
 def head_kernel(
     hid, w, tea, bmap, ups, tok, gh, gx,
     hb, wb, wc, acc, qb, rr, rt, tv, mt, g, st0, st1, st2, perm, gc, ghb, fin, fs,
-    t00, t01, t10, t11, t20, t21, a00, a01, a10, a11, a20, a21,
-    u00, u01, u10, u11, u20, u21, b00, b01, b10, b11, b20, b21,
-    v00, v01, v10, v11, v20, v21, c00, c01, c10, c11, c20, c21,
-    ss, rs, ls, tss, trs, hx, hy,
+    *rest,
 ):
-    tps = ((t00, t01), (t10, t11), (t20, t21))
-    ras = ((a00, a01), (a10, a11), (a20, a21))
-    tbs = ((u00, u01), (u10, u11), (u20, u21))
-    rbs = ((b00, b01), (b10, b11), (b20, b21))
-    tcs = ((v00, v01), (v10, v11), (v20, v21))
-    rcs = ((c00, c01), (c10, c11), (c20, c21))
+    ss, rs, ls, tss, trs, hx, hy = rest[36:]
+
+    def by_unit(n):
+        refs = iter(rest[6 * n : 6 * n + 6])
+        return [[next(refs) for _ in lane] for lane in UNITS]
+
+    tps, ras, tbs, rbs, tcs, rcs = (by_unit(n) for n in range(6))
     dp = lax.axis_index("dp")
     vo = lax.axis_index("vocab")
     x, zl = dp // 2, lax.rem(dp, 2)
@@ -55,6 +66,9 @@
 
     sib = device(x, y, z, o)
     sent = []
+
+    def region(body):
+        pl.when(me >= 0)(body)
 
     def send(src, dst, to):
         k = len(sent)
@@ -192,21 +206,27 @@
     zra, zrb = zring(za), zring(zb)
 
     def mul_x(h, xx):
-        lhs = hb[h, xx, :, :, xs].reshape(192, XW)
-        rows = pl.ds(pl.multiple_of(192 * xx, 64), 192)
-        acc[rows, :] += jnp.dot(lhs, wb[h, xs, :], preferred_element_type=F32)
+        @region
+        def _():
+            lhs = hb[h, xx, :, :, xs].reshape(192, XW)
+            rows = pl.ds(pl.multiple_of(192 * xx, 64), 192)
+            acc[rows, :] += jnp.dot(lhs, wb[h, xs, :], preferred_element_type=F32)
 
     def mul_y(h, yy):
-        lhs = hb[h, :, :, :, ysl(yy)].reshape(768, YW)
-        acc[...] += jnp.dot(lhs, wb[h, ysl(yy), :], preferred_element_type=F32)
+        @region
+        def _():
+            lhs = hb[h, :, :, :, ysl(yy)].reshape(768, YW)
+            acc[...] += jnp.dot(lhs, wb[h, ysl(yy), :], preferred_element_type=F32)
 
     def mul_z(h, zz):
-        q = zq(zz)
-        lhs = hb[h, :, q, :, zs].reshape(192, ZW)
-        res = jnp.dot(lhs, wb[h, zs, :], preferred_element_type=F32)
-        for xx in range(4):
-            rows = pl.ds(pl.multiple_of(192 * xx + 48 * q, 16), 48)
-            acc[rows, :] += res[48 * xx : 48 * xx + 48]
+        @region
+        def _():
+            q = zq(zz)
+            lhs = hb[h, :, q, :, zs].reshape(192, ZW)
+            res = jnp.dot(lhs, wb[h, zs, :], preferred_element_type=F32)
+            for xx in range(4):
+                rows = pl.ds(pl.multiple_of(192 * xx + 48 * q, 16), 48)
+                acc[rows, :] += res[48 * xx : 48 * xx + 48]
 
     def make_perm(p):
         for a in range(6):
@@ -270,6 +290,7 @@
     zrb.start()
     tea_write(tm, ts, 16, 32)
     rr[chip] = mt[chip]
+    give(1, 20)
     yra.forward()
     zra.forward()
     xra.forward()
@@ -281,6 +302,8 @@
     yrb.forward()
     zrb.forward()
     mul_y(c, y)
+    region(lambda: make_perm(0))
+    region(lambda: make_perm(1))
     other.wait()
     arrive(xrb.own)
     mul_x(o, x)
@@ -306,7 +329,7 @@
         mul_z(o, rot(z, d))
     yrb.finish()
     zrb.finish()
-    give(1, 64)
+    give(20, 64)
     mul_y(c, rot(y, 2))
     mul_z(c, rot(z, 2))
     arrive(xra.end, xrb.end)
@@ -349,7 +372,6 @@
             if d + e > 0:
                 to = device(rot(x, d), y, z, c if e == 0 else o)
                 cps.append(send(st0, st1.at[2 * d + e], to))
-    make_perm(0)
     arrive(*cps)
     m, s = merge(st0[...], st1, 8)
     st2[0, 0:8, :] = m
@@ -366,7 +388,6 @@
     )
     whole.wait_recv()
     cross = send(rr.at[:, o], rt, sib)
-    make_perm(1)
     arrive(cross)
     i = lax.broadcasted_iota(jnp.int32, (240, 1), 0)
     j = (i * 1366) >> 16
@@ -389,20 +410,22 @@
     arrive(*cps)
     m, s = merge(st2[0], st2, 16)
     scale = ups[...] * jnp.exp(st0[0:6, :] - m[0:6]) / s[0:6]
+    gsend = []
     for a in range(6):
         rows = slice(128 * a, 128 * a + 128)
         sc = to_col(scale[a : a + 1, :])
         uc = to_col(ups[a : a + 1, :])
-        g[rows, :] = (acc[rows, :] * sc - uc * qb[rows, :].astype(F32)).astype(BF16)
-
-    gsend = []
-    for p in range(2):
-        for a in range(3):
-            rows = slice(256 * a, 256 * a + 256)
-            gc[p, rows, 0:640] = jnp.dot(perm[p, rows, :], g[...], preferred_element_type=F32).astype(BF16)
-        gsend.append(send(gc.at[p, :, pl.ds(0, 640)], gc.at[p, :, pl.ds(640, 640)], sib))
-    arrive(wx)
-    w2copy.wait()
+        g[rows, 0:640] = (acc[rows, :] * sc - uc * qb[rows, :].astype(F32)).astype(BF16)
+        if a % 2 == 1:
+            part = pl.ds(128 * (a - 1), 256)
+            gsend.append(send(g.at[part, pl.ds(0, 640)], g.at[part, pl.ds(640, 640)], sib))
+
+    def order(p):
+        @region
+        def _():
+            for a in range(3):
+                rows = slice(256 * a, 256 * a + 256)
+                gc[p, rows, :] = jnp.dot(perm[p, rows, :], g[...], preferred_element_type=F32).astype(BF16)
 
     co = (x, y, z)
     near = (xn, yn, zn)
@@ -411,28 +434,35 @@
 
     def head_part(n):
         h, k = n // 5, n % 5
-        lhs = hb[h, :, :, :, 512 * k : 512 * k + 512].reshape(768, 512)
-        res = lax.dot_general(lhs, g[...], (((0,), (0,)), ((), ())), preferred_element_type=F32)
-        ghb[512 * n : 512 * n + 512, :] = res.astype(BF16)
+
+        @region
+        def _():
+            lhs = hb[h, :, :, :, 512 * k : 512 * k + 512].reshape(768, 512)
+            res = lax.dot_general(lhs, g[:, 0:640], (((0,), (0,)), ((), ())), preferred_element_type=F32)
+            ghb[512 * n : 512 * n + 512, :] = res.astype(BF16)
+
         cp = pltpu.make_async_copy(ghb.at[pl.ds(512 * n, 512)], gh.at[pl.ds(512 * n, 512)], ls.at[4 + n])
         cp.start()
         return cp
 
-    def partial(p, start, wd):
-        return lax.dot_general(gc[p], wc[start : start + wd, :], nt, preferred_element_type=F32).astype(BF16)
-
-    def stage_a(p, k, res):
-        tp, ra, ax = tps[p][k], ras[p][k], AXES[p][0]
-        for a in range(4):
-            for b in range(4):
-                at = 192 * b + 48 * a if p == 1 else 192 * a + 48 * b
-                tp[a, b] = res[at : at + 48]
+    def partial(p, k):
+        (start, wd), tp, ra, ax = UNITS[p][k], tps[p][k], ras[p][k], AXES[p][0]
+
+        @region
+        def _():
+            res = lax.dot_general(gc[p // 2], wc[start : start + wd, :], nt, preferred_element_type=F32)
+            res = res.astype(BF16)
+            for a in range(4):
+                for b in range(4):
+                    at = 192 * b + 48 * a if p == 1 else 192 * a + 48 * b
+                    tp[a, b] = res[at : at + 48]
+
         v, f = co[ax], near[ax]
-        on, back = ((1, 3), (3, 1))[k]
+        on, back = ((1, 3), (3, 1))[k % 2]
         sa[p, k] = [send(tp.at[rot(v, 2)], ra.at[2], f(on)), send(tp.at[rot(v, back)], ra.at[0], f(back))]
 
     def pass_a(p, k):
-        tp, ra, on = tps[p][k], ras[p][k], (1, 3)[k]
+        tp, ra, on = tps[p][k], ras[p][k], (1, 3)[k % 2]
         arrive(sa[p, k][0])
         ax = AXES[p][0]
         a = rot(co[ax], on)
@@ -465,38 +495,20 @@
         fin[:, start : start + wd] = tcs[p][k][window(co[AXES[p][2]]), :] + rc[0] + rc[1] + rc[2]
 
     heads = []
-    for k in range(2):
-        for p in range(3):
-            if k == 0 and p != 1:
-                arrive(gsend[p // 2])
-            stage_a(p, k, partial(p // 2, *UNITS[p][k]))
-    for p in range(3):
-        pass_a(p, 0)
-    for n in range(2):
-        heads.append(head_part(n))
-    for p in range(3):
-        pass_a(p, 1)
-    for n in range(2, 5):
-        heads.append(head_part(n))
-    for p in range(3):
-        stage_b(p, 0)
-    for n in range(5, 8):
-        heads.append(head_part(n))
-    for p in range(3):
-        stage_b(p, 1)
-    for p in range(3):
-        stage_c(p, 0)
-    for n in range(8, 10):
-        heads.append(head_part(n))
-    for p in range(3):
-        stage_d(p, 0)
-    for p in range(3):
-        stage_c(p, 1)
-    for p in range(3):
-        stage_d(p, 1)
+    arrive(*gsend, wx)
+    w2copy.wait()
+    order(1)
+    steps = {"T": partial, "P": pass_a, "B": stage_b, "C": stage_c, "D": stage_d}
+    for step in [step for group in PLAN for step in group.split()]:
+        if step == "O":
+            order(0)
+        elif step == "H":
+            heads.append(head_part(len(heads)))
+        else:
+            steps[step[0]](int(step[1]), int(step[2]))
     arrive(send(fin, fs, sib))
     for p in range(3):
-        start, wd = min(u[0] for u in UNITS[p]), sum(u[1] for u in UNITS[p])
+        start, wd = UNITS[p][0][0], sum(u[1] for u in UNITS[p])
         odd = lax.rem(co[AXES[p][2]], 2)
         cols = slice(start, start + wd)
         mine, theirs = fin[:, cols], fs[:, cols]
@@ -534,7 +546,7 @@
         pltpu.VMEM((64, 32, 128), BF16),
         pltpu.VMEM((32, 6, HALF), BF16),
         pltpu.VMEM((64, 2, 32, 128), BF16),
-        pltpu.VMEM((768, 640), BF16),
+        pltpu.VMEM((768, 1280), BF16),
         pltpu.VMEM((16, 128), F32),
         pltpu.VMEM((8, 16, 128), F32),
         pltpu.VMEM((16, 16, 128), F32),
@@ -549,8 +561,8 @@
         *per_unit(lambda wd: (3, 48, wd), BF16),
         *per_unit(lambda wd: (48, wd), F32),
         *per_unit(lambda wd: (3, 16, wd), F32),
-        pltpu.SemaphoreType.DMA((160,)),
-        pltpu.SemaphoreType.DMA((160,)),
+        pltpu.SemaphoreType.DMA((192,)),
+        pltpu.SemaphoreType.DMA((192,)),
         pltpu.SemaphoreType.DMA((17,)),
         pltpu.SemaphoreType.DMA,
         pltpu.SemaphoreType.DMA,

time: 102 us -> 105 us (1.029)
  Pallas kernels: 94.5 us -> 97.4 us
    pallas_call x1, Pallas kernels: 94.5 us -> 97.4 us  [shards(): pl.pallas_call(head_kernel, out_shape=(jax.ShapeDtypeStruct((5120, 640),...]
where the time goes in v4:
time: 105 us
  Pallas kernels  97.4 us (93%)
  local copies, waits for them, and re-layouts  6.88 us (7%)
    pallas_call x1, Pallas kernels, shards(): pl.pallas_call(head_kernel, out_shape=(jax.ShapeDtypeStruct((5120, 640),...  97.4 us
    unnamed x4, local copies, waits for them, and re-layouts  6.88 us

profile of v4, /device:TPU:1, one launch (start us, length us, event | category | flops | bytes accessed | tf_op | source)
XLA Modules:
  0.0 104.9 jit_solution(551456175813660840)
XLA Ops:
  0.6 97.4 %head_backward.1 = (bf16[5120,640]{1,0:T(8,128)(2,1)}, bf16[6,5120]{1,0:T(8,128)(2,1)}) custom-call(bf16[2,48,5120]{2,1,0:T(8,128)(2,1)} %bitcast.5, bf16[2,2560,640]{2,1,0:T(8,128)(2,1)} %bitcast.4, bf16[6,81920]{1,0:T(8,128)(2,1)} %tea.1, s32[32]{0:T(128)} %bmap.1, f32[6,128]{1,0:T(8,128)} %bitcast.6, s32[6,128]{1,0:T(8,128)} %bitcast.7), custom_call_target="tpu_custom_call" | custom-call | tf_op jit(solution)/shard_map/head_backward/pallas_call | solution.py:572
  98.0 0.0 copy-start
  98.0 6.2 %copy.10 = bf16[5120,640]{1,0:T(8,128)(2,1)} copy(bf16[5120,640]{1,0:T(8,128)(2,1)} %get-tuple-element.4) | data formatting | bytes 13107200
  104.3 0.0 copy-done
  104.3 0.6 copy.11
Async XLA Ops:
  98.0 6.3 %copy-start = (bf16[6,5120]{1,0:T(8,128)(2,1)S(1)}, bf16[6,5120]{1,0:T(8,128)(2,1)}, u32[]{:S(2)}) copy-start(bf16[6,5120]{1,0:T(8,128)(2,1)} %get-tuple-element.5) | copy-start | bytes 184324
